TPU v7x, 32 devices: a whole 2x2x4 slice. The times are simulated.
32 devices in a mesh: req: 16 (over z, y, x), tp: 2 (over core).
Axes of the slice: x: 2, y: 2, z: 4, core: 2. Of those that a mesh axis runs over, the one named last changes fastest.
Arguments:
- hidden_in: bfloat16 [256, 2048], P('req'), may hold values from -6 to 6
- query: bfloat16 [256, 2048], P('req', 'tp'), may hold values from -200 to 200
- new_kv: bfloat16 [256, 4096], P('req', 'tp'), may hold values from -6 to 6
- pool_cache: bfloat16 [1280, 32, 4096], P('req', None, 'tp'), may hold values from -7 to 7
- prompt_table: int32 [32, 24], P('req'), may hold values from 0 to 79, as said below
- prompt_len: int32 [32], P('req'), may hold values from 32 to 768
- req_group: int32 [256], P('req'), may hold values from 0 to 1, as said below
- cont_table: int32 [256, 2], P('req'), may hold values from 0 to 79, as said below
- cont_len: int32 [256], P('req'), may hold values from 1 to 63
- migration: int32 [96, 2], P('req'), may hold values from 0 to 15, as said below
- diff_lambda: float32 [8], P('tp'), may hold values from 0.2 to 0.8
- out_weight: bfloat16 [2048, 2048], P('tp'), may hold values from -0.125 to 0.125
- norm_gain: float32 [2048], replicated, may hold values from 0.1 to 1.9
Outputs:
- hidden_out: bfloat16 [256, 2048], P('req')
- normed_out: bfloat16 [256, 2048], P('req')
- arrived: bfloat16 [128, 64, 4096], P('req', None, 'tp')
Inputs may be any that keep to these rules, and one draw needn't show every extreme that they name: `prompt_table`: entries are pages local to the row's index of req; with cont_table, each of a device's 80 pages appears exactly once. `cont_table`: local pages, each page of a device once together with prompt_table. `req_group`: A group index local to the device; every group of a device has a request. `migration`: each device lists 6 rows: a distinct local request slot and a destination offset 1 to 4 along req (with wrap); at most 2 rows of a device share an offset, and that many is reached.
All inputs are finite; a program needn't handle non-finite values.
Results may differ from a plain program's by a relative error of at most 0.012.
Values may be sent and summed in bfloat16 or wider, within the bound.
No kernel may reach another device: no remote copies, remote signals or barrier semaphores. Data moves between devices by JAX's collectives and lax.ppermute only.
A program may use at most 128 MiB of HBM per device.

v0:
```python
import functools

import jax
import jax.numpy as jnp
from jax import lax
from jax.experimental import pallas as pl
from jax.experimental.pallas import tpu as pltpu
from jax.sharding import PartitionSpec as P

MIG_REACH = 4
MIG_CAP = 2
KEY = 128
ROWS = 16

SMEM = pl.BlockSpec(memory_space=pltpu.SMEM)
VMEM = pl.BlockSpec(memory_space=pltpu.VMEM)
HBM = pl.BlockSpec(memory_space=pltpu.HBM)
VMEM_BYTES = 40 * 1024 * 1024
SMALL_VMEM_BYTES = 8 * 1024 * 1024


def pinned(*arrays):
    return [pltpu.with_memory_space_constraint(array, pltpu.HBM) for array in arrays]


def shifted(value, axis, steps):
    count = lax.axis_size(axis)
    pairs = [(source, (source + steps) % count) for source in range(count)]
    return lax.ppermute(value, axis, pairs)


def send_kernel(offsets, table_in, length_in, migration_in, new_in, pool, *refs):
    outs = refs[: len(offsets)]
    table, length, migration, holder, new_held, new_rows, sems, small_sems = refs[len(offsets) :]
    small = [
        pltpu.make_async_copy(source, target, small_sems.at[n])
        for n, (source, target) in enumerate(
            zip((table_in, length_in, migration_in, new_in), (table, length, migration, new_held))
        )
    ]
    for copy in small:
        copy.start()
    for copy in small[:3]:
        copy.wait()
    entries = migration.shape[1]
    pages, page = table.shape[0], pool.shape[1]
    for place in range(MIG_REACH * MIG_CAP):
        holder[place] = -1
    odd = lax.rem(lax.axis_index("req"), 2)
    where = []
    for n, (on_even, on_odd) in enumerate(offsets):
        offset = on_even + odd * (on_odd - on_even)
        for i in range(MIG_CAP):
            where.append((n * MIG_CAP + i, (offset - 1) * MIG_CAP + i, outs[n].at[i]))
    for e in range(entries):
        rank = jnp.int32(0)
        for before in range(e):
            rank += (migration[1, before] == migration[1, e]).astype(jnp.int32)
        holder[(migration[1, e] - 1) * MIG_CAP + rank] = migration[0, e]

    def last_of(place):
        slot = holder[place]
        return jnp.where(slot >= 0, length[jnp.maximum(slot, 0)], -1)

    def block_copy(n, place, out, low):
        source = pool.at[table[low // page, jnp.maximum(holder[place], 0)], pl.ds(low % page, ROWS)]
        return pltpu.make_async_copy(source, out.at[pl.ds(low, ROWS)], sems.at[n, low // ROWS])

    lows = range(0, pages * page, ROWS)
    for n, place, out in where:
        for low in lows:

            @pl.when(last_of(place) >= low)
            def _():
                block_copy(n, place, out, low).start()

    for n, place, out in where:
        for low in lows:

            @pl.when(last_of(place) < low)
            def _():
                out[pl.ds(low, ROWS)] = jnp.zeros((ROWS, out.shape[1]), out.dtype)

    small[3].wait()
    new_rows[...] = new_held[...].astype(jnp.float32)
    for n, place, out in where:
        last = last_of(place)
        safe = jnp.maximum(holder[place], 0)
        for low in lows:

            @pl.when(last >= low)
            def _():
                block_copy(n, place, out, low).wait()

            @pl.when((last >= low) & (last < low + ROWS))
            def _():
                held = out[pl.ds(low, ROWS)].astype(jnp.float32)
                pos = low + lax.broadcasted_iota(jnp.int32, held.shape, 0)
                new = jnp.where(pos == last, new_rows[pl.ds(safe, 1)], 0.0)
                out[pl.ds(low, ROWS)] = jnp.where(pos < last, held, new).astype(out.dtype)


def send_slots(offsets, cont_table, cont_len, migration, new_kv, pool):
    span = cont_table.shape[0] * pool.shape[1]
    width = pool.shape[2]
    return pl.pallas_call(
        functools.partial(send_kernel, offsets),
        out_shape=[jax.ShapeDtypeStruct((MIG_CAP, span, width), pool.dtype)] * len(offsets),
        in_specs=[HBM] * 5,
        out_specs=[VMEM] * len(offsets),
        scratch_shapes=[
            pltpu.SMEM(cont_table.shape, jnp.int32),
            pltpu.SMEM(cont_len.shape, jnp.int32),
            pltpu.SMEM(migration.shape, jnp.int32),
            pltpu.SMEM((MIG_REACH * MIG_CAP,), jnp.int32),
            pltpu.VMEM(new_kv.shape, new_kv.dtype),
            pltpu.VMEM(new_kv.shape, jnp.float32),
            pltpu.SemaphoreType.DMA((len(offsets) * MIG_CAP, span // ROWS)),
            pltpu.SemaphoreType.DMA((4,)),
        ],
        compiler_params=pltpu.CompilerParams(vmem_limit_bytes=VMEM_BYTES),
        name="send_slots",
    )(*pinned(cont_table, cont_len, migration, new_kv, pool))


def column(values, count):
    rows = lax.broadcasted_iota(jnp.int32, (count, 1), 0)
    out = jnp.zeros((count, 1), jnp.int32)
    for r in range(count):
        out = jnp.where(rows == r, values[r], out)
    return out


def attention_kernel(low, prompt_table, prompt_len, req_group, cont_table, cont_len, lam, query, new_ref, *refs):
    prior = refs[:-6]
    weight, pool, out, held, weight_held, sems = refs[-6:]
    groups, prompt_pages = prompt_table.shape
    cont_pages, reqs = cont_table.shape
    page = pool.shape[1]
    span = prompt_pages * page
    own = cont_pages * page
    start = groups * span
    head_width = pool.shape[2] // lam.shape[0]
    value_width = head_width - 2 * KEY
    width = held.shape[1]
    heads = width // head_width
    columns = pl.ds(low * head_width, width)

    for g in range(groups):

        @pl.loop(0, prompt_pages)
        def _(j):
            at = pl.multiple_of(g * span + j * page, page)
            pltpu.make_async_copy(pool.at[prompt_table[g, j], :, columns], held.at[pl.ds(at, page)], sems.at[0]).start()

    @pl.loop(0, reqs)
    def _(r):
        for j in range(cont_pages):
            at = pl.multiple_of(start + r * own + j * page, page)
            pltpu.make_async_copy(pool.at[cont_table[j, r], :, columns], held.at[pl.ds(at, page)], sems.at[0]).start()

    rows = pl.ds(low * value_width, weight_held.shape[0])
    weight_copy = pltpu.make_async_copy(weight.at[rows], weight_held, sems.at[1])
    weight_copy.start()

    group_of = column(req_group, reqs)
    length_of = column(cont_len, reqs)
    biases = []
    pos = lax.broadcasted_iota(jnp.int32, (reqs, span), 1)
    for g in range(groups):
        live = (group_of == g) & (pos < prompt_len[g])
        biases.append(jnp.where(live, 0.0, -1e30))
    key = lax.broadcasted_iota(jnp.int32, (reqs, reqs * own), 1)
    pos = key - own * lax.broadcasted_iota(jnp.int32, (reqs, reqs * own), 0)
    biases.append(jnp.where((pos >= 0) & (pos < length_of), 0.0, -1e30))
    live = jnp.concatenate(biases, axis=1) == 0.0

    pltpu.make_async_copy(held, held, sems.at[0]).wait()

    scale = KEY**-0.5
    mixed = []
    for h in range(heads):
        first = h * head_width
        weights, new_weights = [], []
        for i in range(2):
            q = query[:, pl.ds((2 * (low + h) + i) * KEY, KEY)]
            cols = pl.ds(first + i * KEY, KEY)
            new_cols = pl.ds(low * head_width + first + i * KEY, KEY)
            score = lax.dot_general(
                q, held[:, cols], (((1,), (1,)), ((), ())), preferred_element_type=jnp.float32
            )
            score = jnp.where(live, score * scale, -1e30)
            new = jnp.sum(q.astype(jnp.float32) * new_ref[:, new_cols].astype(jnp.float32), axis=1, keepdims=True) * scale
            top = jnp.maximum(jnp.max(score, axis=1, keepdims=True), new)
            score = jnp.exp(score - top)
            new = jnp.exp(new - top)
            inverse = 1.0 / (jnp.sum(score, axis=1, keepdims=True) + new)
            weights.append((score * inverse).astype(jnp.bfloat16))
            new_weights.append((new * inverse).astype(jnp.bfloat16).astype(jnp.float32))
        cols = pl.ds(first + 2 * KEY, value_width)
        mixture = jnp.dot(jnp.concatenate(weights, axis=0), held[:, cols], preferred_element_type=jnp.float32)
        new_value = new_ref[:, pl.ds(low * head_width + first + 2 * KEY, value_width)].astype(jnp.float32)
        one = mixture[:reqs] + new_weights[0] * new_value
        two = mixture[reqs:] + new_weights[1] * new_value
        diff = one - lam[low + h] * two
        norm = lax.rsqrt(jnp.mean(diff * diff, axis=1, keepdims=True) + 1e-05)
        mixed.append((diff * norm * 0.8).astype(jnp.bfloat16))
    weight_copy.wait()
    mixed = jnp.concatenate(mixed, axis=1)
    product = jnp.dot(mixed, weight_held[...], preferred_element_type=jnp.float32)
    for part in prior:
        product = product + part[...]
    out[...] = product.astype(out.dtype)


def attention(query, new_kv, pool, prompt_table, prompt_len, req_group, cont_table, cont_len, lam, weight, low, high, prior):
    reqs = query.shape[0]
    page = pool.shape[1]
    heads = lam.shape[0]
    keys = (prompt_table.size + cont_table.size) * page
    width = pool.shape[2] // heads * (high - low)
    rows = weight.shape[0] // heads * (high - low)
    return pl.pallas_call(
        functools.partial(attention_kernel, low),
        out_shape=jax.ShapeDtypeStruct((reqs, weight.shape[1]), jnp.bfloat16 if high == heads else jnp.float32),
        in_specs=[SMEM] * 6 + [VMEM] * (2 + len(prior)) + [HBM, HBM],
        out_specs=VMEM,
        scratch_shapes=[
            pltpu.VMEM((keys, width), pool.dtype),
            pltpu.VMEM((rows, weight.shape[1]), weight.dtype),
            pltpu.SemaphoreType.DMA((2,)),
        ],
        compiler_params=pltpu.CompilerParams(vmem_limit_bytes=VMEM_BYTES),
        cost_estimate=pl.CostEstimate(
            flops=4 * reqs * keys * width + 2 * reqs * rows * weight.shape[1],
            bytes_accessed=2 * (keys * width + rows * weight.shape[1]),
            transcendentals=reqs * keys * 2 * (high - low),
        ),
        name="attention",
    )(prompt_table, prompt_len, req_group, cont_table, cont_len, lam, query, new_kv, *prior, *pinned(weight, pool))


def finish_kernel(count, hidden, gain, *refs):
    parts = refs[:count]
    hidden_out, normed_out = refs[count:]
    total = parts[0][...].astype(jnp.float32)
    for part in parts[1:]:
        total = total + part[...].astype(jnp.float32)
    summed = hidden[...].astype(jnp.float32) + total
    norm = lax.rsqrt(jnp.mean(summed * summed, axis=1, keepdims=True) + 1e-05)
    hidden_out[...] = summed.astype(hidden_out.dtype)
    normed_out[...] = (summed * norm * gain[...]).astype(normed_out.dtype)


def finish(hidden, gain, parts):
    shape = jax.ShapeDtypeStruct(hidden.shape, jnp.bfloat16)
    return pl.pallas_call(
        functools.partial(finish_kernel, len(parts)),
        out_shape=[shape, shape],
        in_specs=[VMEM] * (2 + len(parts)),
        out_specs=[VMEM, VMEM],
        compiler_params=pltpu.CompilerParams(vmem_limit_bytes=SMALL_VMEM_BYTES),
        name="finish",
    )(hidden, gain.reshape(1, -1), *parts)


def gather_kernel(choose, count, *refs):
    parts, out, sems = refs[:count], refs[-2], refs[-1]
    copies = [
        (pltpu.make_async_copy(parts[part], out.at[pl.ds(place, MIG_CAP)], sems.at[n]), taken)
        for n, (place, part, taken) in enumerate(choose())
    ]
    for copy, taken in copies:
        pl.when(taken)(copy.start)
    for copy, taken in copies:
        pl.when(taken)(copy.wait)


def arrive(parts, choose, rest=None):
    slots = MIG_REACH * MIG_CAP
    extra = [] if rest is None else pinned(rest)
    return pl.pallas_call(
        functools.partial(gather_kernel, choose, len(parts)),
        out_shape=jax.ShapeDtypeStruct((slots,) + parts[0].shape[1:], parts[0].dtype),
        in_specs=[VMEM] * len(parts) + [HBM] * len(extra),
        out_specs=HBM,
        scratch_shapes=[pltpu.SemaphoreType.DMA((2 * MIG_REACH,))],
        input_output_aliases={len(parts): 0} if extra else {},
        compiler_params=pltpu.CompilerParams(vmem_limit_bytes=SMALL_VMEM_BYTES),
        name="arrive",
    )(*parts, *extra)


def routed(value, targets):
    count, width = lax.axis_size("req"), lax.axis_size("tp")
    pairs = []
    for s in range(count):
        for t in range(width):
            target = targets(s, t % 2)
            if target is not None:
                target = target % count
                pairs.append((s * width + t, target * width + (t ^ 1 if target == s else t)))
    return lax.ppermute(value, ("req", "tp"), pairs)


def turn(s, steps):
    return s - s % MIG_REACH + (s + steps) % MIG_REACH


def route_early(s, odd):
    if s % 2 == 0:
        return s + 1
    return turn(s, 3) if odd else s + 3


def route_late(s, odd):
    return s + 3 if s % 2 == 0 else s + 1


def lift_two(s, odd):
    return s + MIG_REACH if s % MIG_REACH < 2 else s


def lift_early(s, odd):
    return s + MIG_REACH if odd and s % 2 == 0 else None


def choose_straight():
    return [(n * MIG_CAP, n, True) for n in range(MIG_REACH)]


def where_am_i():
    col = lax.rem(lax.axis_index("req"), MIG_REACH)
    odd = lax.rem(col, 2) == 1
    odd_core = lax.rem(lax.axis_index("tp"), 2) == 1
    return col, odd, jnp.logical_not(odd), odd_core


def choose_sooner():
    col, odd, even, odd_core = where_am_i()
    return [(0, 2, odd), (2, 0, col >= 2), (2, 1, col < 2), (4, 2, even & jnp.logical_not(odd_core)), (6, 3, True)]


def choose_later():
    col, odd, even, odd_core = where_am_i()
    return [(0, 1, even), (4, 1, odd), (4, 0, even & odd_core)]


def can_relay():
    count = lax.axis_size("req")
    return MIG_REACH == 4 and count % MIG_REACH == 0 and count > MIG_REACH and lax.axis_size("tp") % 2 == 0


def shards(
    hidden_in,
    query,
    new_kv,
    pool_cache,
    prompt_table,
    prompt_len,
    req_group,
    cont_table,
    cont_len,
    migration,
    diff_lambda,
    out_weight,
    norm_gain,
):
    cont_table, migration = cont_table.T, migration.T
    heads = diff_lambda.shape[0]
    half = heads // 2
    attend = functools.partial(
        attention, query, new_kv, pool_cache, prompt_table, prompt_len, req_group, cont_table, cont_len, diff_lambda, out_weight
    )
    send = (cont_table, cont_len, migration, new_kv, pool_cache)
    prior = [attend(0, half, [])] if half else []
    if can_relay():
        two, four, early = send_slots(((2, 2), (4, 4), (1, 3)), *send)
        two = routed(two, lambda s, odd: turn(s, 2))
        four = shifted(four, "req", 4)
        early = routed(early, route_early)
        prior, later_len = lax.optimization_barrier((prior, cont_len))
        (late,) = send_slots(((3, 1),), cont_table, later_len, *send[2:])
        prior, two, late = lax.optimization_barrier((prior, two, late))
        two_up = routed(two, lift_two)
        late = routed(late, route_late)
        early_up = routed(early, lift_early)
    else:
        outgoing = send_slots(tuple((o, o) for o in range(1, MIG_REACH + 1)), *send)
        arrived = arrive([shifted(part, "req", o + 1) for o, part in enumerate(outgoing)], choose_straight)
    partial = attend(half, heads, prior)
    if lax.axis_size("tp") == 2:
        parts = [partial, shifted(partial, "tp", 1)]
    else:
        parts = [lax.psum(partial, "tp")]
    hidden_out, normed_out = finish(hidden_in, norm_gain, parts)
    if can_relay():
        sooner = arrive((two, two_up, early, four), choose_sooner)
        arrived = arrive((early_up, late), choose_later, sooner)
    return (hidden_out, normed_out, arrived)


def solution(mesh):
    placed = (
        P("req", None),
        P("req", "tp"),
        P("req", "tp"),
        P("req", None, "tp"),
        P("req", None),
        P("req"),
        P("req"),
        P("req", None),
        P("req"),
        P("req", None),
        P("tp"),
        P("tp", None),
        P(),
    )
    return jax.shard_map(
        shards,
        mesh=mesh,
        in_specs=placed,
        out_specs=(P("req", None), P("req", None), P("req", None, "tp")),
        check_vma=False,
    )
```

profile of v0, /device:TPU:1, one launch (start us, length us, event | category | flops | bytes accessed | tf_op | source)
XLA Modules:
  0.0 40.0 jit_solution(11416890434776173198)
XLA Ops:
  0.6 0.0 copy-start
  0.6 0.0 copy-start.2
  0.7 0.0 copy-start.4
  0.7 0.0 copy-start.6
  0.7 2.3 %send_slots.2 = (bf16[2,64,2048]{2,1,0:T(8,128)(2,1)S(1)}, bf16[2,64,2048]{2,1,0:T(8,128)(2,1)S(1)}, bf16[2,64,2048]{2,1,0:T(8,128)(2,1)S(1)}) custom-call(s32[2,16]{1,0:T(2,128)} %bitcast.3, s32[16]{0:T(128)} %cont_len.3, s32[2,6]{1,0:T(2,128)} %bitcast.8, bf16[16,2048]{1,0:T(8,128)(2,1)} %new_ref.3, bf16[80,32,2048]{2,1,0:T(8,128)(2,1)} %refs_2_.1), custom_call_target="tpu_custom_call" | custom-call | tf_op jit(solution)/shard_map/send_slots/pallas_call | solution.py:106
  3.0 2.2 %collective-permute-start = (bf16[2,64,2048]{2,1,0:T(8,128)(2,1)S(1)}, bf16[2,64,2048]{2,1,0:T(8,128)(2,1)S(1)}, u32[]{:S(2)}, u32[]{:S(2)}) collective-permute-start(bf16[2,64,2048]{2,1,0:T(8,128)(2,1)S(1)} %get-tuple-element.14), channel_id=1, source_target_pairs={{0,4},{1,5},{2,6},{3,7},{4,0},{5,1},{6,2},{7,3},{8,12},{9,13},{10,... | collective-permute-start | bytes 1572872 | tf_op jit(solution)/shard_map/ppermute | solution.py:303
  5.2 1.2 %collective-permute-start.2 = (bf16[2,64,2048]{2,1,0:T(8,128)(2,1)S(1)}, bf16[2,64,2048]{2,1,0:T(8,128)(2,1)S(1)}, u32[]{:S(2)}, u32[]{:S(2)}) collective-permute-start(bf16[2,64,2048]{2,1,0:T(8,128)(2,1)S(1)} %get-tuple-element.19), channel_id=1, source_target_pairs={{0,2},{1,3},{2,8},{3,1},{4,6},{5,7},{6,12},{7,5},{8,10},{9,11},{10... | collective-permute-start | bytes 1572872 | tf_op jit(solution)/shard_map/ppermute | solution.py:303
  6.4 1.3 %collective-permute-start.6 = (bf16[2,64,2048]{2,1,0:T(8,128)(2,1)S(1)}, bf16[2,64,2048]{2,1,0:T(8,128)(2,1)S(1)}, u32[]{:S(2)}, u32[]{:S(2)}) collective-permute-start(bf16[2,64,2048]{2,1,0:T(8,128)(2,1)S(1)} %get-tuple-element.22), channel_id=1, source_target_pairs={{0,8},{2,10},{4,12},{6,14},{8,16},{10,18},{12,20},{14,22},{16,24},... | collective-permute-start | bytes 1572872 | tf_op jit(solution)/shard_map/ppermute | solution.py:29
  7.8 0.0 copy-done.2
  7.8 5.7 %attention.2.refs_0_ = f32[16,2048]{1,0:T(8,128)S(1)} custom-call(s32[2,24]{1,0:T(2,128)S(1)} %copy-done.9, s32[2]{0:T(128)S(1)} %copy-done.10, s32[16]{0:T(128)S(1)} %copy-done.11, s32[2,16]{1,0:T(2,128)S(1)} %bitcast.5, s32[16]{0:T(128)S(1)} %copy-done.6, f32[4]{0:T(128)S(1)} %copy-done.12, bf16[16,1024]{1,0:T(8,128)(2,1)S(1)} %copy-done.2, ...), custom_call_target="tpu_custom_call" | custom-call | flops 201326592 | bytes 7340032 | tf_op jit(solution)/shard_map/attention/pallas_call | solution.py:223
  13.6 0.0 copy-start.1
  13.6 0.0 copy-start.5
  13.6 0.0 copy-start.7
  13.6 2.0 %send_slots.3 = bf16[2,64,2048]{2,1,0:T(8,128)(2,1)S(1)} custom-call(s32[2,16]{1,0:T(2,128)} %bitcast.4, s32[16]{0:T(128)} %cont_len.3, s32[2,6]{1,0:T(2,128)} %bitcast.9, bf16[16,2048]{1,0:T(8,128)(2,1)} %new_ref.3, bf16[80,32,2048]{2,1,0:T(8,128)(2,1)} %refs_2_.1), custom_call_target="tpu_custom_call" | custom-call | tf_op jit(solution)/shard_map/send_slots/pallas_call | solution.py:106
  15.6 0.0 copy-start.3
  15.6 0.0 copy-start.8
  15.6 1.3 %collective-permute-done.refs_0_ = bf16[2,64,2048]{2,1,0:T(8,128)(2,1)S(1)} collective-permute-done((bf16[2,64,2048]{2,1,0:T(8,128)(2,1)S(1)}, bf16[2,64,2048]{2,1,0:T(8,128)(2,1)S(1)}, u32[]{:S(2)}, u32[]{:S(2)}) %collective-permute-start) | collective-permute-done | bytes 524320 | tf_op jit(solution)/shard_map/ppermute | solution.py:303
  16.9 1.2 %collective-permute-start.5 = (bf16[2,64,2048]{2,1,0:T(8,128)(2,1)S(1)}, bf16[2,64,2048]{2,1,0:T(8,128)(2,1)S(1)}, u32[]{:S(2)}, u32[]{:S(2)}) collective-permute-start(bf16[2,64,2048]{2,1,0:T(8,128)(2,1)S(1)} %collective-permute-done.refs_0_), channel_id=1, source_target_pairs={{0,8},{1,9},{2,10},{3,11},{4,5},{5,4},{6,7},{7,6},{8,16},{9,17},{1... | collective-permute-start | bytes 1572872 | tf_op jit(solution)/shard_map/ppermute | solution.py:303
  18.1 2.4 %collective-permute-start.4 = (bf16[2,64,2048]{2,1,0:T(8,128)(2,1)S(1)}, bf16[2,64,2048]{2,1,0:T(8,128)(2,1)S(1)}, u32[]{:S(2)}, u32[]{:S(2)}) collective-permute-start(bf16[2,64,2048]{2,1,0:T(8,128)(2,1)S(1)} %send_slots.3), channel_id=1, source_target_pairs={{0,6},{1,7},{2,4},{3,5},{4,10},{5,11},{6,8},{7,9},{8,14},{9,15},{1... | collective-permute-start | bytes 1572872 | tf_op jit(solution)/shard_map/ppermute | solution.py:303
  20.5 0.0 collective-permute-done.2.refs_2_
  20.5 3.2 %collective-permute-start.3 = (bf16[2,64,2048]{2,1,0:T(8,128)(2,1)S(1)}, bf16[2,64,2048]{2,1,0:T(8,128)(2,1)S(1)}, u32[]{:S(2)}, u32[]{:S(2)}) collective-permute-start(bf16[2,64,2048]{2,1,0:T(8,128)(2,1)S(1)} %collective-permute-done.2.refs_2_), channel_id=1, source_target_pairs={{1,9},{5,13},{9,17},{13,21},{17,25},{21,29},{25,1},{29,5}} | collective-permute-start | bytes 1572872 | tf_op jit(solution)/shard_map/ppermute | solution.py:303
  23.8 5.7 %attention.3.refs_0_ = bf16[16,2048]{1,0:T(8,128)(2,1)S(1)} custom-call(s32[2,24]{1,0:T(2,128)S(1)} %copy-done.9, s32[2]{0:T(128)S(1)} %copy-done.10, s32[16]{0:T(128)S(1)} %copy-done.11, s32[2,16]{1,0:T(2,128)S(1)} %bitcast.6, s32[16]{0:T(128)S(1)} %copy-done.7, f32[4]{0:T(128)S(1)} %copy-done.12, bf16[16,1024]{1,0:T(8,128)(2,1)S(1)} %copy-done.2, ...), custom_call_target="tpu_custom_call" | custom-call | flops 201326592 | bytes 7340032 | tf_op jit(solution)/shard_map/attention/pallas_call | solution.py:223
  29.5 0.1 collective-permute-start.1
  29.6 1.2 %collective-permute-done.1.refs_1_ = bf16[16,2048]{1,0:T(8,128)(2,1)S(1)} collective-permute-done((bf16[16,2048]{1,0:T(8,128)(2,1)S(1)}, bf16[16,2048]{1,0:T(8,128)(2,1)S(1)}, u32[]{:S(2)}, u32[]{:S(2)}) %collective-permute-start.1) | collective-permute-done | bytes 65568 | tf_op jit(solution)/shard_map/ppermute | solution.py:29
  30.8 0.0 copy-done.8
  30.8 0.8 %finish.1 = (bf16[16,2048]{1,0:T(8,128)(2,1)}, bf16[16,2048]{1,0:T(8,128)(2,1)}) custom-call(bf16[16,2048]{1,0:T(8,128)(2,1)S(1)} %copy-done.3, f32[1,2048]{1,0:T(1,128)S(1)} %bitcast.7, bf16[16,2048]{1,0:T(8,128)(2,1)S(1)} %attention.3.refs_0_, bf16[16,2048]{1,0:T(8,128)(2,1)S(1)} %collective-permute-done.1.refs_1_), custom_call_target="tpu_custom_call" | custom-call | tf_op jit(solution)/shard_map/finish/pallas_call | solution.py:257
  31.6 0.0 collective-permute-done.6.refs_3_
  31.6 1.0 %collective-permute-done.5.refs_1_ = bf16[2,64,2048]{2,1,0:T(8,128)(2,1)S(1)} collective-permute-done((bf16[2,64,2048]{2,1,0:T(8,128)(2,1)S(1)}, bf16[2,64,2048]{2,1,0:T(8,128)(2,1)S(1)}, u32[]{:S(2)}, u32[]{:S(2)}) %collective-permute-start.5) | collective-permute-done | bytes 524320 | tf_op jit(solution)/shard_map/ppermute | solution.py:303
  32.6 1.0 %arrive.2.refs_2_ = bf16[8,64,2048]{2,1,0:T(8,128)(2,1)} custom-call(bf16[2,64,2048]{2,1,0:T(8,128)(2,1)S(1)} %collective-permute-done.refs_0_, bf16[2,64,2048]{2,1,0:T(8,128)(2,1)S(1)} %collective-permute-done.5.refs_1_, bf16[2,64,2048]{2,1,0:T(8,128)(2,1)S(1)} %collective-permute-done.2.refs_2_, bf16[2,64,2048]{2,1,0:T(8,128)(2,1)S(1)} %collective-permute-done.6.refs_3_), custom_call_target="tpu_custom_call" | custom-call | tf_op jit(solution)/shard_map/arrive/pallas_call | solution.py:282
  33.6 2.5 %collective-permute-done.4.refs_1_ = bf16[2,64,2048]{2,1,0:T(8,128)(2,1)S(1)} collective-permute-done((bf16[2,64,2048]{2,1,0:T(8,128)(2,1)S(1)}, bf16[2,64,2048]{2,1,0:T(8,128)(2,1)S(1)}, u32[]{:S(2)}, u32[]{:S(2)}) %collective-permute-start.4) | collective-permute-done | bytes 524320 | tf_op jit(solution)/shard_map/ppermute | solution.py:303
  36.1 2.9 %collective-permute-done.3.refs_0_ = bf16[2,64,2048]{2,1,0:T(8,128)(2,1)S(1)} collective-permute-done((bf16[2,64,2048]{2,1,0:T(8,128)(2,1)S(1)}, bf16[2,64,2048]{2,1,0:T(8,128)(2,1)S(1)}, u32[]{:S(2)}, u32[]{:S(2)}) %collective-permute-start.3) | collective-permute-done | bytes 524320 | tf_op jit(solution)/shard_map/ppermute | solution.py:303
  38.9 1.0 %arrive.3 = bf16[8,64,2048]{2,1,0:T(8,128)(2,1)} custom-call(bf16[2,64,2048]{2,1,0:T(8,128)(2,1)S(1)} %collective-permute-done.3.refs_0_, bf16[2,64,2048]{2,1,0:T(8,128)(2,1)S(1)} %collective-permute-done.4.refs_1_, bf16[8,64,2048]{2,1,0:T(8,128)(2,1)} %arrive.2.refs_2_), custom_call_target="tpu_custom_call", output_to_operand_aliasing={{}: (2, {})} | custom-call | tf_op jit(solution)/shard_map/arrive/pallas_call | solution.py:282
  (15 shorter events, 0.0 us)
Async XLA Ops:
  0.6 7.2 %copy-start = (bf16[16,2048]{1,0:T(8,128)(2,1)S(1)}, bf16[16,2048]{1,0:T(8,128)(2,1)}, u32[]{:S(2)}) copy-start(bf16[16,2048]{1,0:T(8,128)(2,1)} %new_ref.3) | copy-start | bytes 196612
  0.6 7.1 %copy-start.2 = (bf16[16,1024]{1,0:T(8,128)(2,1)S(1)}, bf16[16,1024]{1,0:T(8,128)(2,1)}, u32[]{:S(2)}) copy-start(bf16[16,1024]{1,0:T(8,128)(2,1)} %query.3) | copy-start | bytes 98308
  0.7 7.1 %copy-start.4 = (s32[16,2]{0,1:T(2,128)S(1)}, s32[16,2]{0,1:T(2,128)}, u32[]{:S(2)}) copy-start(s32[16,2]{0,1:T(2,128)} %param.20) | copy-start | bytes 388
  0.7 7.1 %copy-start.6 = (s32[16]{0:T(128)S(1)}, s32[16]{0:T(128)}, u32[]{:S(2)}) copy-start(s32[16]{0:T(128)} %cont_len.3) | copy-start | bytes 196
  0.7 7.1 %copy-start.9 = (s32[2,24]{1,0:T(2,128)S(1)}, s32[2,24]{1,0:T(2,128)}, u32[]{:S(2)}) copy-start(s32[2,24]{1,0:T(2,128)} %prompt_table.3) | copy-start | bytes 580
  0.7 7.1 %copy-start.10 = (s32[2]{0:T(128)S(1)}, s32[2]{0:T(128)}, u32[]{:S(2)}) copy-start(s32[2]{0:T(128)} %prompt_len.3) | copy-start | bytes 28
  0.7 7.1 %copy-start.11 = (s32[16]{0:T(128)S(1)}, s32[16]{0:T(128)}, u32[]{:S(2)}) copy-start(s32[16]{0:T(128)} %req_group.3) | copy-start | bytes 196
  0.7 7.1 %copy-start.12 = (f32[4]{0:T(128)S(1)}, f32[4]{0:T(128)}, u32[]{:S(2)}) copy-start(f32[4]{0:T(128)} %lam.3) | copy-start | bytes 52
  3.0 13.8 %collective-permute-start = (bf16[2,64,2048]{2,1,0:T(8,128)(2,1)S(1)}, bf16[2,64,2048]{2,1,0:T(8,128)(2,1)S(1)}, u32[]{:S(2)}, u32[]{:S(2)}) collective-permute-start(bf16[2,64,2048]{2,1,0:T(8,128)(2,1)S(1)} %get-tuple-element.14), channel_id=1, source_target_pairs={{0,4},{1,5},{2,6},{3,7},{4,0},{5,1},{6,2},{7,3},{8,12},{9,13},{10,... | collective-permute-start | bytes 1572872 | tf_op jit(solution)/shard_map/ppermute | solution.py:303
  5.2 15.3 %collective-permute-start.2 = (bf16[2,64,2048]{2,1,0:T(8,128)(2,1)S(1)}, bf16[2,64,2048]{2,1,0:T(8,128)(2,1)S(1)}, u32[]{:S(2)}, u32[]{:S(2)}) collective-permute-start(bf16[2,64,2048]{2,1,0:T(8,128)(2,1)S(1)} %get-tuple-element.19), channel_id=1, source_target_pairs={{0,2},{1,3},{2,8},{3,1},{4,6},{5,7},{6,12},{7,5},{8,10},{9,11},{10... | collective-permute-start | bytes 1572872 | tf_op jit(solution)/shard_map/ppermute | solution.py:303
  6.4 25.1 %collective-permute-start.6 = (bf16[2,64,2048]{2,1,0:T(8,128)(2,1)S(1)}, bf16[2,64,2048]{2,1,0:T(8,128)(2,1)S(1)}, u32[]{:S(2)}, u32[]{:S(2)}) collective-permute-start(bf16[2,64,2048]{2,1,0:T(8,128)(2,1)S(1)} %get-tuple-element.22), channel_id=1, source_target_pairs={{0,8},{2,10},{4,12},{6,14},{8,16},{10,18},{12,20},{14,22},{16,24},... | collective-permute-start | bytes 1572872 | tf_op jit(solution)/shard_map/ppermute | solution.py:29
  13.6 10.2 %copy-start.1 = (bf16[16,2048]{1,0:T(8,128)(2,1)S(1)}, bf16[16,2048]{1,0:T(8,128)(2,1)}, u32[]{:S(2)}) copy-start(bf16[16,2048]{1,0:T(8,128)(2,1)} %new_ref.3) | copy-start | bytes 196612
  13.6 10.2 %copy-start.5 = (s32[16,2]{0,1:T(2,128)S(1)}, s32[16,2]{0,1:T(2,128)}, u32[]{:S(2)}) copy-start(s32[16,2]{0,1:T(2,128)} %param.20) | copy-start | bytes 388
  13.6 10.2 %copy-start.7 = (s32[16]{0:T(128)S(1)}, s32[16]{0:T(128)}, u32[]{:S(2)}) copy-start(s32[16]{0:T(128)} %cont_len.3) | copy-start | bytes 196
  15.6 15.2 %copy-start.3 = (bf16[16,2048]{1,0:T(8,128)(2,1)S(1)}, bf16[16,2048]{1,0:T(8,128)(2,1)}, u32[]{:S(2)}) copy-start(bf16[16,2048]{1,0:T(8,128)(2,1)} %hidden.1) | copy-start | bytes 196612
  15.6 15.2 %copy-start.8 = (f32[2048]{0:T(1024)S(1)}, f32[2048]{0:T(1024)}, u32[]{:S(2)}) copy-start(f32[2048]{0:T(1024)} %param.25) | copy-start | bytes 24580
  16.9 15.7 %collective-permute-start.5 = (bf16[2,64,2048]{2,1,0:T(8,128)(2,1)S(1)}, bf16[2,64,2048]{2,1,0:T(8,128)(2,1)S(1)}, u32[]{:S(2)}, u32[]{:S(2)}) collective-permute-start(bf16[2,64,2048]{2,1,0:T(8,128)(2,1)S(1)} %collective-permute-done.refs_0_), channel_id=1, source_target_pairs={{0,8},{1,9},{2,10},{3,11},{4,5},{5,4},{6,7},{7,6},{8,16},{9,17},{1... | collective-permute-start | bytes 1572872 | tf_op jit(solution)/shard_map/ppermute | solution.py:303
  18.1 18.0 %collective-permute-start.4 = (bf16[2,64,2048]{2,1,0:T(8,128)(2,1)S(1)}, bf16[2,64,2048]{2,1,0:T(8,128)(2,1)S(1)}, u32[]{:S(2)}, u32[]{:S(2)}) collective-permute-start(bf16[2,64,2048]{2,1,0:T(8,128)(2,1)S(1)} %send_slots.3), channel_id=1, source_target_pairs={{0,6},{1,7},{2,4},{3,5},{4,10},{5,11},{6,8},{7,9},{8,14},{9,15},{1... | collective-permute-start | bytes 1572872 | tf_op jit(solution)/shard_map/ppermute | solution.py:303
  20.5 18.4 %collective-permute-start.3 = (bf16[2,64,2048]{2,1,0:T(8,128)(2,1)S(1)}, bf16[2,64,2048]{2,1,0:T(8,128)(2,1)S(1)}, u32[]{:S(2)}, u32[]{:S(2)}) collective-permute-start(bf16[2,64,2048]{2,1,0:T(8,128)(2,1)S(1)} %collective-permute-done.2.refs_2_), channel_id=1, source_target_pairs={{1,9},{5,13},{9,17},{13,21},{17,25},{21,29},{25,1},{29,5}} | collective-permute-start | bytes 1572872 | tf_op jit(solution)/shard_map/ppermute | solution.py:303
  29.5 1.3 %collective-permute-start.1 = (bf16[16,2048]{1,0:T(8,128)(2,1)S(1)}, bf16[16,2048]{1,0:T(8,128)(2,1)S(1)}, u32[]{:S(2)}, u32[]{:S(2)}) collective-permute-start(bf16[16,2048]{1,0:T(8,128)(2,1)S(1)} %attention.3.refs_0_), channel_id=1, source_target_pairs={{0,1},{1,0},{2,3},{3,2},{4,5},{5,4},{6,7},{7,6},{8,9},{9,8},{10,11... | collective-permute-start | bytes 196616 | tf_op jit(solution)/shard_map/ppermute | solution.py:29
where the time goes:
time: 40.5 us; the launch traced here: 40 us
  Pallas kernels  18.5 us (46%)
  starting transfers between devices  11.7 us (29%)
  waiting for transfers between devices  8.83 us (22%)
  between operations  0.86 us (2%)
    pallas_call x2, Pallas kernels, attention(): pl.pallas_call(functools.partial(attention_kernel, low), out_shape=jax.Sh...  11.4 us
    ppermute x5, starting transfers between devices, routed(): return lax.ppermute(value, ('req', 'tp'), pairs)  10.3 us
    ppermute x5, waiting for transfers between devices, routed(): return lax.ppermute(value, ('req', 'tp'), pairs)  7.59 us
    pallas_call x2, Pallas kernels, send_slots(): pl.pallas_call(functools.partial(send_kernel, offsets), out_shape=[jax.Sh...  4.29 us
    pallas_call x2, Pallas kernels, arrive(): pl.pallas_call(functools.partial(gather_kernel, choose, len(parts)), out_...  2.07 us
    ppermute x2, starting transfers between devices, shifted(): return lax.ppermute(value, axis, pairs)  1.42 us
    ppermute x2, waiting for transfers between devices, shifted(): return lax.ppermute(value, axis, pairs)  1.24 us
  transfers between devices with their start and end apart: 7, of which 5 were waited for; matrix products, arithmetic and copies ran while one was open for 0% of the time, Pallas kernels for 38%

commit v1 on v0

--- a/solution.py
+++ b/solution.py
@@ -266,10 +266,14 @@
 
 def gather_kernel(choose, count, *refs):
     parts, out, sems = refs[:count], refs[-2], refs[-1]
-    copies = [
-        (pltpu.make_async_copy(parts[part], out.at[pl.ds(place, MIG_CAP)], sems.at[n]), taken)
-        for n, (place, part, taken) in enumerate(choose())
-    ]
+    copies = []
+    for place, part, taken in choose():
+        slots, span = parts[part].shape[:2]
+        for at in range(slots):
+            for half in range(2):
+                rows = pl.ds(half * span // 2, span // 2)
+                source, target = parts[part].at[at, rows], out.at[place + at, rows]
+                copies.append((pltpu.make_async_copy(source, target, sems.at[len(copies)]), taken))
     for copy, taken in copies:
         pl.when(taken)(copy.start)
     for copy, taken in copies:
@@ -284,7 +288,7 @@
         out_shape=jax.ShapeDtypeStruct((slots,) + parts[0].shape[1:], parts[0].dtype),
         in_specs=[VMEM] * len(parts) + [HBM] * len(extra),
         out_specs=HBM,
-        scratch_shapes=[pltpu.SemaphoreType.DMA((2 * MIG_REACH,))],
+        scratch_shapes=[pltpu.SemaphoreType.DMA((4 * MIG_REACH * MIG_CAP,))],
         input_output_aliases={len(parts): 0} if extra else {},
         compiler_params=pltpu.CompilerParams(vmem_limit_bytes=SMALL_VMEM_BYTES),
         name="arrive",

time: 40.5 us -> 40.7 us (level)
  Pallas kernels: 18.5 us -> 19 us
where the time goes in v1:
time: 40.7 us; the launch traced here: 40.2 us
  Pallas kernels  19 us (47%)
  starting transfers between devices  11.5 us (28%)
  waiting for transfers between devices  8.71 us (21%)
  between operations  0.86 us (2%)
    pallas_call x2, Pallas kernels, attention(): pl.pallas_call(functools.partial(attention_kernel, low), out_shape=jax.Sh...  11.4 us
    ppermute x5, starting transfers between devices, routed(): return lax.ppermute(value, ('req', 'tp'), pairs)  10.2 us
    ppermute x5, waiting for transfers between devices, routed(): return lax.ppermute(value, ('req', 'tp'), pairs)  7.46 us
    pallas_call x2, Pallas kernels, send_slots(): pl.pallas_call(functools.partial(send_kernel, offsets), out_shape=[jax.Sh...  4.38 us
    pallas_call x2, Pallas kernels, arrive(): pl.pallas_call(functools.partial(gather_kernel, choose, len(parts)), out_...  2.48 us
    ppermute x2, starting transfers between devices, shifted(): return lax.ppermute(value, axis, pairs)  1.3 us
    ppermute x2, waiting for transfers between devices, shifted(): return lax.ppermute(value, axis, pairs)  1.24 us
  transfers between devices with their start and end apart: 7, of which 5 were waited for; matrix products, arithmetic and copies ran while one was open for 0% of the time, Pallas kernels for 38%

profile of v1, /device:TPU:1, one launch (start us, length us, event | category | flops | bytes accessed | tf_op | source)
XLA Modules:
  0.0 40.2 jit_solution(6288461494926032740)
XLA Ops:
  0.6 0.0 copy-start
  0.6 0.0 copy-start.2
  0.7 0.0 copy-start.4
  0.7 0.0 copy-start.6
  0.7 2.3 %send_slots.2 = (bf16[2,64,2048]{2,1,0:T(8,128)(2,1)S(1)}, bf16[2,64,2048]{2,1,0:T(8,128)(2,1)S(1)}, bf16[2,64,2048]{2,1,0:T(8,128)(2,1)S(1)}) custom-call(s32[2,16]{1,0:T(2,128)} %bitcast.3, s32[16]{0:T(128)} %cont_len.3, s32[2,6]{1,0:T(2,128)} %bitcast.8, bf16[16,2048]{1,0:T(8,128)(2,1)} %new_ref.3, bf16[80,32,2048]{2,1,0:T(8,128)(2,1)} %refs_2_.1), custom_call_target="tpu_custom_call" | custom-call | tf_op jit(solution)/shard_map/send_slots/pallas_call | solution.py:106
  3.0 2.2 %collective-permute-start = (bf16[2,64,2048]{2,1,0:T(8,128)(2,1)S(1)}, bf16[2,64,2048]{2,1,0:T(8,128)(2,1)S(1)}, u32[]{:S(2)}, u32[]{:S(2)}) collective-permute-start(bf16[2,64,2048]{2,1,0:T(8,128)(2,1)S(1)} %get-tuple-element.14), channel_id=1, source_target_pairs={{0,4},{1,5},{2,6},{3,7},{4,0},{5,1},{6,2},{7,3},{8,12},{9,13},{10,... | collective-permute-start | bytes 1572872 | tf_op jit(solution)/shard_map/ppermute | solution.py:307
  5.2 1.2 %collective-permute-start.2 = (bf16[2,64,2048]{2,1,0:T(8,128)(2,1)S(1)}, bf16[2,64,2048]{2,1,0:T(8,128)(2,1)S(1)}, u32[]{:S(2)}, u32[]{:S(2)}) collective-permute-start(bf16[2,64,2048]{2,1,0:T(8,128)(2,1)S(1)} %get-tuple-element.19), channel_id=1, source_target_pairs={{0,2},{1,3},{2,8},{3,1},{4,6},{5,7},{6,12},{7,5},{8,10},{9,11},{10... | collective-permute-start | bytes 1572872 | tf_op jit(solution)/shard_map/ppermute | solution.py:307
  6.5 1.2 %collective-permute-start.6 = (bf16[2,64,2048]{2,1,0:T(8,128)(2,1)S(1)}, bf16[2,64,2048]{2,1,0:T(8,128)(2,1)S(1)}, u32[]{:S(2)}, u32[]{:S(2)}) collective-permute-start(bf16[2,64,2048]{2,1,0:T(8,128)(2,1)S(1)} %get-tuple-element.22), channel_id=1, source_target_pairs={{0,8},{2,10},{4,12},{6,14},{8,16},{10,18},{12,20},{14,22},{16,24},... | collective-permute-start | bytes 1572872 | tf_op jit(solution)/shard_map/ppermute | solution.py:29
  7.7 0.0 copy-done
  7.7 0.0 copy-done.9
  7.8 5.7 %attention.2.refs_0_ = f32[16,2048]{1,0:T(8,128)S(1)} custom-call(s32[2,24]{1,0:T(2,128)S(1)} %copy-done.9, s32[2]{0:T(128)S(1)} %copy-done.10, s32[16]{0:T(128)S(1)} %copy-done.11, s32[2,16]{1,0:T(2,128)S(1)} %bitcast.5, s32[16]{0:T(128)S(1)} %copy-done.6, f32[4]{0:T(128)S(1)} %copy-done.12, bf16[16,1024]{1,0:T(8,128)(2,1)S(1)} %copy-done.2, ...), custom_call_target="tpu_custom_call" | custom-call | flops 201326592 | bytes 7340032 | tf_op jit(solution)/shard_map/attention/pallas_call | solution.py:223
  13.5 0.0 copy-start.1
  13.5 0.0 copy-start.5
  13.5 0.0 copy-start.7
  13.5 2.1 %send_slots.3 = bf16[2,64,2048]{2,1,0:T(8,128)(2,1)S(1)} custom-call(s32[2,16]{1,0:T(2,128)} %bitcast.4, s32[16]{0:T(128)} %cont_len.3, s32[2,6]{1,0:T(2,128)} %bitcast.9, bf16[16,2048]{1,0:T(8,128)(2,1)} %new_ref.3, bf16[80,32,2048]{2,1,0:T(8,128)(2,1)} %refs_2_.1), custom_call_target="tpu_custom_call" | custom-call | tf_op jit(solution)/shard_map/send_slots/pallas_call | solution.py:106
  15.6 0.0 copy-start.3
  15.6 0.0 copy-start.8
  15.6 1.3 %collective-permute-done.refs_0_ = bf16[2,64,2048]{2,1,0:T(8,128)(2,1)S(1)} collective-permute-done((bf16[2,64,2048]{2,1,0:T(8,128)(2,1)S(1)}, bf16[2,64,2048]{2,1,0:T(8,128)(2,1)S(1)}, u32[]{:S(2)}, u32[]{:S(2)}) %collective-permute-start) | collective-permute-done | bytes 524320 | tf_op jit(solution)/shard_map/ppermute | solution.py:307
  16.9 1.1 %collective-permute-start.5 = (bf16[2,64,2048]{2,1,0:T(8,128)(2,1)S(1)}, bf16[2,64,2048]{2,1,0:T(8,128)(2,1)S(1)}, u32[]{:S(2)}, u32[]{:S(2)}) collective-permute-start(bf16[2,64,2048]{2,1,0:T(8,128)(2,1)S(1)} %collective-permute-done.refs_0_), channel_id=1, source_target_pairs={{0,8},{1,9},{2,10},{3,11},{4,5},{5,4},{6,7},{7,6},{8,16},{9,17},{1... | collective-permute-start | bytes 1572872 | tf_op jit(solution)/shard_map/ppermute | solution.py:307
  18.0 2.5 %collective-permute-start.4 = (bf16[2,64,2048]{2,1,0:T(8,128)(2,1)S(1)}, bf16[2,64,2048]{2,1,0:T(8,128)(2,1)S(1)}, u32[]{:S(2)}, u32[]{:S(2)}) collective-permute-start(bf16[2,64,2048]{2,1,0:T(8,128)(2,1)S(1)} %send_slots.3), channel_id=1, source_target_pairs={{0,6},{1,7},{2,4},{3,5},{4,10},{5,11},{6,8},{7,9},{8,14},{9,15},{1... | collective-permute-start | bytes 1572872 | tf_op jit(solution)/shard_map/ppermute | solution.py:307
  20.5 0.0 collective-permute-done.2.refs_2_
  20.5 3.1 %collective-permute-start.3 = (bf16[2,64,2048]{2,1,0:T(8,128)(2,1)S(1)}, bf16[2,64,2048]{2,1,0:T(8,128)(2,1)S(1)}, u32[]{:S(2)}, u32[]{:S(2)}) collective-permute-start(bf16[2,64,2048]{2,1,0:T(8,128)(2,1)S(1)} %collective-permute-done.2.refs_2_), channel_id=1, source_target_pairs={{1,9},{5,13},{9,17},{13,21},{17,25},{21,29},{25,1},{29,5}} | collective-permute-start | bytes 1572872 | tf_op jit(solution)/shard_map/ppermute | solution.py:307
  23.7 5.7 %attention.3.refs_0_ = bf16[16,2048]{1,0:T(8,128)(2,1)S(1)} custom-call(s32[2,24]{1,0:T(2,128)S(1)} %copy-done.9, s32[2]{0:T(128)S(1)} %copy-done.10, s32[16]{0:T(128)S(1)} %copy-done.11, s32[2,16]{1,0:T(2,128)S(1)} %bitcast.6, s32[16]{0:T(128)S(1)} %copy-done.7, f32[4]{0:T(128)S(1)} %copy-done.12, bf16[16,1024]{1,0:T(8,128)(2,1)S(1)} %copy-done.2, ...), custom_call_target="tpu_custom_call" | custom-call | flops 201326592 | bytes 7340032 | tf_op jit(solution)/shard_map/attention/pallas_call | solution.py:223
  29.4 0.1 collective-permute-start.1
  29.5 1.2 %collective-permute-done.1.refs_1_ = bf16[16,2048]{1,0:T(8,128)(2,1)S(1)} collective-permute-done((bf16[16,2048]{1,0:T(8,128)(2,1)S(1)}, bf16[16,2048]{1,0:T(8,128)(2,1)S(1)}, u32[]{:S(2)}, u32[]{:S(2)}) %collective-permute-start.1) | collective-permute-done | bytes 65568 | tf_op jit(solution)/shard_map/ppermute | solution.py:29
  30.7 0.8 %finish.1 = (bf16[16,2048]{1,0:T(8,128)(2,1)}, bf16[16,2048]{1,0:T(8,128)(2,1)}) custom-call(bf16[16,2048]{1,0:T(8,128)(2,1)S(1)} %copy-done.3, f32[1,2048]{1,0:T(1,128)S(1)} %bitcast.7, bf16[16,2048]{1,0:T(8,128)(2,1)S(1)} %attention.3.refs_0_, bf16[16,2048]{1,0:T(8,128)(2,1)S(1)} %collective-permute-done.1.refs_1_), custom_call_target="tpu_custom_call" | custom-call | tf_op jit(solution)/shard_map/finish/pallas_call | solution.py:257
  31.5 0.0 collective-permute-done.6.refs_3_
  31.5 1.0 %collective-permute-done.5.refs_1_ = bf16[2,64,2048]{2,1,0:T(8,128)(2,1)S(1)} collective-permute-done((bf16[2,64,2048]{2,1,0:T(8,128)(2,1)S(1)}, bf16[2,64,2048]{2,1,0:T(8,128)(2,1)S(1)}, u32[]{:S(2)}, u32[]{:S(2)}) %collective-permute-start.5) | collective-permute-done | bytes 524320 | tf_op jit(solution)/shard_map/ppermute | solution.py:307
  32.5 1.2 %arrive.2.refs_2_ = bf16[8,64,2048]{2,1,0:T(8,128)(2,1)} custom-call(bf16[2,64,2048]{2,1,0:T(8,128)(2,1)S(1)} %collective-permute-done.refs_0_, bf16[2,64,2048]{2,1,0:T(8,128)(2,1)S(1)} %collective-permute-done.5.refs_1_, bf16[2,64,2048]{2,1,0:T(8,128)(2,1)S(1)} %collective-permute-done.2.refs_2_, bf16[2,64,2048]{2,1,0:T(8,128)(2,1)S(1)} %collective-permute-done.6.refs_3_), custom_call_target="tpu_custom_call" | custom-call | tf_op jit(solution)/shard_map/arrive/pallas_call | solution.py:286
  33.7 2.3 %collective-permute-done.4.refs_1_ = bf16[2,64,2048]{2,1,0:T(8,128)(2,1)S(1)} collective-permute-done((bf16[2,64,2048]{2,1,0:T(8,128)(2,1)S(1)}, bf16[2,64,2048]{2,1,0:T(8,128)(2,1)S(1)}, u32[]{:S(2)}, u32[]{:S(2)}) %collective-permute-start.4) | collective-permute-done | bytes 524320 | tf_op jit(solution)/shard_map/ppermute | solution.py:307
  36.0 2.9 %collective-permute-done.3.refs_0_ = bf16[2,64,2048]{2,1,0:T(8,128)(2,1)S(1)} collective-permute-done((bf16[2,64,2048]{2,1,0:T(8,128)(2,1)S(1)}, bf16[2,64,2048]{2,1,0:T(8,128)(2,1)S(1)}, u32[]{:S(2)}, u32[]{:S(2)}) %collective-permute-start.3) | collective-permute-done | bytes 524320 | tf_op jit(solution)/shard_map/ppermute | solution.py:307
  38.9 1.2 %arrive.3 = bf16[8,64,2048]{2,1,0:T(8,128)(2,1)} custom-call(bf16[2,64,2048]{2,1,0:T(8,128)(2,1)S(1)} %collective-permute-done.3.refs_0_, bf16[2,64,2048]{2,1,0:T(8,128)(2,1)S(1)} %collective-permute-done.4.refs_1_, bf16[8,64,2048]{2,1,0:T(8,128)(2,1)} %arrive.2.refs_2_), custom_call_target="tpu_custom_call", output_to_operand_aliasing={{}: (2, {})} | custom-call | tf_op jit(solution)/shard_map/arrive/pallas_call | solution.py:286
  (15 shorter events, 0.0 us)
Async XLA Ops:
  0.6 7.1 %copy-start = (bf16[16,2048]{1,0:T(8,128)(2,1)S(1)}, bf16[16,2048]{1,0:T(8,128)(2,1)}, u32[]{:S(2)}) copy-start(bf16[16,2048]{1,0:T(8,128)(2,1)} %new_ref.3) | copy-start | bytes 196612
  0.6 7.1 %copy-start.2 = (bf16[16,1024]{1,0:T(8,128)(2,1)S(1)}, bf16[16,1024]{1,0:T(8,128)(2,1)}, u32[]{:S(2)}) copy-start(bf16[16,1024]{1,0:T(8,128)(2,1)} %query.3) | copy-start | bytes 98308
  0.7 7.1 %copy-start.4 = (s32[16,2]{0,1:T(2,128)S(1)}, s32[16,2]{0,1:T(2,128)}, u32[]{:S(2)}) copy-start(s32[16,2]{0,1:T(2,128)} %param.20) | copy-start | bytes 388
  0.7 7.0 %copy-start.6 = (s32[16]{0:T(128)S(1)}, s32[16]{0:T(128)}, u32[]{:S(2)}) copy-start(s32[16]{0:T(128)} %cont_len.3) | copy-start | bytes 196
  0.7 7.0 %copy-start.9 = (s32[2,24]{1,0:T(2,128)S(1)}, s32[2,24]{1,0:T(2,128)}, u32[]{:S(2)}) copy-start(s32[2,24]{1,0:T(2,128)} %prompt_table.3) | copy-start | bytes 580
  0.7 7.0 %copy-start.10 = (s32[2]{0:T(128)S(1)}, s32[2]{0:T(128)}, u32[]{:S(2)}) copy-start(s32[2]{0:T(128)} %prompt_len.3) | copy-start | bytes 28
  0.7 7.0 %copy-start.11 = (s32[16]{0:T(128)S(1)}, s32[16]{0:T(128)}, u32[]{:S(2)}) copy-start(s32[16]{0:T(128)} %req_group.3) | copy-start | bytes 196
  0.7 7.0 %copy-start.12 = (f32[4]{0:T(128)S(1)}, f32[4]{0:T(128)}, u32[]{:S(2)}) copy-start(f32[4]{0:T(128)} %lam.3) | copy-start | bytes 52
  3.0 13.9 %collective-permute-start = (bf16[2,64,2048]{2,1,0:T(8,128)(2,1)S(1)}, bf16[2,64,2048]{2,1,0:T(8,128)(2,1)S(1)}, u32[]{:S(2)}, u32[]{:S(2)}) collective-permute-start(bf16[2,64,2048]{2,1,0:T(8,128)(2,1)S(1)} %get-tuple-element.14), channel_id=1, source_target_pairs={{0,4},{1,5},{2,6},{3,7},{4,0},{5,1},{6,2},{7,3},{8,12},{9,13},{10,... | collective-permute-start | bytes 1572872 | tf_op jit(solution)/shard_map/ppermute | solution.py:307
  5.2 15.3 %collective-permute-start.2 = (bf16[2,64,2048]{2,1,0:T(8,128)(2,1)S(1)}, bf16[2,64,2048]{2,1,0:T(8,128)(2,1)S(1)}, u32[]{:S(2)}, u32[]{:S(2)}) collective-permute-start(bf16[2,64,2048]{2,1,0:T(8,128)(2,1)S(1)} %get-tuple-element.19), channel_id=1, source_target_pairs={{0,2},{1,3},{2,8},{3,1},{4,6},{5,7},{6,12},{7,5},{8,10},{9,11},{10... | collective-permute-start | bytes 1572872 | tf_op jit(solution)/shard_map/ppermute | solution.py:307
  6.5 25.0 %collective-permute-start.6 = (bf16[2,64,2048]{2,1,0:T(8,128)(2,1)S(1)}, bf16[2,64,2048]{2,1,0:T(8,128)(2,1)S(1)}, u32[]{:S(2)}, u32[]{:S(2)}) collective-permute-start(bf16[2,64,2048]{2,1,0:T(8,128)(2,1)S(1)} %get-tuple-element.22), channel_id=1, source_target_pairs={{0,8},{2,10},{4,12},{6,14},{8,16},{10,18},{12,20},{14,22},{16,24},... | collective-permute-start | bytes 1572872 | tf_op jit(solution)/shard_map/ppermute | solution.py:29
  13.5 10.2 %copy-start.1 = (bf16[16,2048]{1,0:T(8,128)(2,1)S(1)}, bf16[16,2048]{1,0:T(8,128)(2,1)}, u32[]{:S(2)}) copy-start(bf16[16,2048]{1,0:T(8,128)(2,1)} %new_ref.3) | copy-start | bytes 196612
  13.5 10.2 %copy-start.5 = (s32[16,2]{0,1:T(2,128)S(1)}, s32[16,2]{0,1:T(2,128)}, u32[]{:S(2)}) copy-start(s32[16,2]{0,1:T(2,128)} %param.20) | copy-start | bytes 388
  13.5 10.2 %copy-start.7 = (s32[16]{0:T(128)S(1)}, s32[16]{0:T(128)}, u32[]{:S(2)}) copy-start(s32[16]{0:T(128)} %cont_len.3) | copy-start | bytes 196
  15.6 15.2 %copy-start.3 = (bf16[16,2048]{1,0:T(8,128)(2,1)S(1)}, bf16[16,2048]{1,0:T(8,128)(2,1)}, u32[]{:S(2)}) copy-start(bf16[16,2048]{1,0:T(8,128)(2,1)} %hidden.1) | copy-start | bytes 196612
  15.6 15.1 %copy-start.8 = (f32[2048]{0:T(1024)S(1)}, f32[2048]{0:T(1024)}, u32[]{:S(2)}) copy-start(f32[2048]{0:T(1024)} %param.25) | copy-start | bytes 24580
  16.9 15.6 %collective-permute-start.5 = (bf16[2,64,2048]{2,1,0:T(8,128)(2,1)S(1)}, bf16[2,64,2048]{2,1,0:T(8,128)(2,1)S(1)}, u32[]{:S(2)}, u32[]{:S(2)}) collective-permute-start(bf16[2,64,2048]{2,1,0:T(8,128)(2,1)S(1)} %collective-permute-done.refs_0_), channel_id=1, source_target_pairs={{0,8},{1,9},{2,10},{3,11},{4,5},{5,4},{6,7},{7,6},{8,16},{9,17},{1... | collective-permute-start | bytes 1572872 | tf_op jit(solution)/shard_map/ppermute | solution.py:307
  18.0 18.0 %collective-permute-start.4 = (bf16[2,64,2048]{2,1,0:T(8,128)(2,1)S(1)}, bf16[2,64,2048]{2,1,0:T(8,128)(2,1)S(1)}, u32[]{:S(2)}, u32[]{:S(2)}) collective-permute-start(bf16[2,64,2048]{2,1,0:T(8,128)(2,1)S(1)} %send_slots.3), channel_id=1, source_target_pairs={{0,6},{1,7},{2,4},{3,5},{4,10},{5,11},{6,8},{7,9},{8,14},{9,15},{1... | collective-permute-start | bytes 1572872 | tf_op jit(solution)/shard_map/ppermute | solution.py:307
  20.5 18.4 %collective-permute-start.3 = (bf16[2,64,2048]{2,1,0:T(8,128)(2,1)S(1)}, bf16[2,64,2048]{2,1,0:T(8,128)(2,1)S(1)}, u32[]{:S(2)}, u32[]{:S(2)}) collective-permute-start(bf16[2,64,2048]{2,1,0:T(8,128)(2,1)S(1)} %collective-permute-done.2.refs_2_), channel_id=1, source_target_pairs={{1,9},{5,13},{9,17},{13,21},{17,25},{21,29},{25,1},{29,5}} | collective-permute-start | bytes 1572872 | tf_op jit(solution)/shard_map/ppermute | solution.py:307
  29.4 1.3 %collective-permute-start.1 = (bf16[16,2048]{1,0:T(8,128)(2,1)S(1)}, bf16[16,2048]{1,0:T(8,128)(2,1)S(1)}, u32[]{:S(2)}, u32[]{:S(2)}) collective-permute-start(bf16[16,2048]{1,0:T(8,128)(2,1)S(1)} %attention.3.refs_0_), channel_id=1, source_target_pairs={{0,1},{1,0},{2,3},{3,2},{4,5},{5,4},{6,7},{7,6},{8,9},{9,8},{10,11... | collective-permute-start | bytes 196616 | tf_op jit(solution)/shard_map/ppermute | solution.py:29

commit v2 on v0

--- a/solution.py
+++ b/solution.py
@@ -58,46 +58,47 @@
             rank += (migration[1, before] == migration[1, e]).astype(jnp.int32)
         holder[(migration[1, e] - 1) * MIG_CAP + rank] = migration[0, e]
 
-    def last_of(place):
-        slot = holder[place]
-        return jnp.where(slot >= 0, length[jnp.maximum(slot, 0)], -1)
-
-    def block_copy(n, place, out, low):
-        source = pool.at[table[low // page, jnp.maximum(holder[place], 0)], pl.ds(low % page, ROWS)]
-        return pltpu.make_async_copy(source, out.at[pl.ds(low, ROWS)], sems.at[n, low // ROWS])
-
-    lows = range(0, pages * page, ROWS)
-    for n, place, out in where:
-        for low in lows:
-
-            @pl.when(last_of(place) >= low)
-            def _():
-                block_copy(n, place, out, low).start()
-
-    for n, place, out in where:
-        for low in lows:
-
-            @pl.when(last_of(place) < low)
-            def _():
-                out[pl.ds(low, ROWS)] = jnp.zeros((ROWS, out.shape[1]), out.dtype)
+    slots = [holder[place] for _, place, _ in where]
+    lasts = [jnp.where(slot >= 0, length[jnp.maximum(slot, 0)], -1) for slot in slots]
+    slots = [jnp.maximum(slot, 0) for slot in slots]
+    blocks = [lax.div(last + ROWS, ROWS) for last in lasts]
+    items = [(n, out, *rest) for (n, _, out), *rest in zip(where, slots, lasts, blocks)]
+
+    def rows_of(block):
+        return pl.ds(pl.multiple_of(block * ROWS, ROWS), ROWS)
+
+    def block_copy(n, out, slot, block):
+        per_page = page // ROWS
+        source = pool.at[table[lax.div(block, per_page), slot], rows_of(lax.rem(block, per_page))]
+        return pltpu.make_async_copy(source, out.at[rows_of(block)], sems.at[n, block])
+
+    for n, out, slot, last, used in items:
+
+        @pl.loop(0, used)
+        def _(block):
+            block_copy(n, out, slot, block).start()
+
+    for n, out, slot, last, used in items:
+
+        @pl.loop(used, pages * page // ROWS)
+        def _(block):
+            out[rows_of(block)] = jnp.zeros((ROWS, out.shape[1]), out.dtype)
 
     small[3].wait()
     new_rows[...] = new_held[...].astype(jnp.float32)
-    for n, place, out in where:
-        last = last_of(place)
-        safe = jnp.maximum(holder[place], 0)
-        for low in lows:
-
-            @pl.when(last >= low)
-            def _():
-                block_copy(n, place, out, low).wait()
-
-            @pl.when((last >= low) & (last < low + ROWS))
-            def _():
-                held = out[pl.ds(low, ROWS)].astype(jnp.float32)
-                pos = low + lax.broadcasted_iota(jnp.int32, held.shape, 0)
-                new = jnp.where(pos == last, new_rows[pl.ds(safe, 1)], 0.0)
-                out[pl.ds(low, ROWS)] = jnp.where(pos < last, held, new).astype(out.dtype)
+    for n, out, slot, last, used in items:
+
+        @pl.loop(0, used)
+        def _(block):
+            block_copy(n, out, slot, block).wait()
+
+        @pl.when(used > 0)
+        def _():
+            rows = rows_of(used - 1)
+            held = out[rows].astype(jnp.float32)
+            pos = (used - 1) * ROWS + lax.broadcasted_iota(jnp.int32, held.shape, 0)
+            new = jnp.where(pos == last, new_rows[pl.ds(slot, 1)], 0.0)
+            out[rows] = jnp.where(pos < last, held, new).astype(out.dtype)
 
 
 def send_slots(offsets, cont_table, cont_len, migration, new_kv, pool):

time: 40.5 us -> 40.6 us (level)
  no operation moved by 1% of the time
where the time goes in v2:
time: 40.6 us; the launch traced here: 40 us
  Pallas kernels  18.6 us (46%)
  starting transfers between devices  11.6 us (29%)
  waiting for transfers between devices  8.81 us (22%)
  between operations  0.86 us (2%)
    pallas_call x2, Pallas kernels, attention(): pl.pallas_call(functools.partial(attention_kernel, low), out_shape=jax.Sh...  11.4 us
    ppermute x5, starting transfers between devices, routed(): return lax.ppermute(value, ('req', 'tp'), pairs)  10.2 us
    ppermute x5, waiting for transfers between devices, routed(): return lax.ppermute(value, ('req', 'tp'), pairs)  7.56 us
    pallas_call x2, Pallas kernels, send_slots(): pl.pallas_call(functools.partial(send_kernel, offsets), out_shape=[jax.Sh...  4.36 us
    pallas_call x2, Pallas kernels, arrive(): pl.pallas_call(functools.partial(gather_kernel, choose, len(parts)), out_...  2.07 us
    ppermute x2, starting transfers between devices, shifted(): return lax.ppermute(value, axis, pairs)  1.39 us
    ppermute x2, waiting for transfers between devices, shifted(): return lax.ppermute(value, axis, pairs)  1.24 us
  transfers between devices with their start and end apart: 7, of which 5 were waited for; matrix products, arithmetic and copies ran while one was open for 0% of the time, Pallas kernels for 38%

profile of v2, /device:TPU:1, one launch (start us, length us, event | category | flops | bytes accessed | tf_op | source)
XLA Modules:
  0.0 40.0 jit_solution(6293334258075715813)
XLA Ops:
  0.6 0.0 copy-start
  0.6 0.0 copy-start.2
  0.7 0.0 copy-start.4
  0.7 0.0 copy-start.6
  0.7 2.3 %send_slots.2 = (bf16[2,64,2048]{2,1,0:T(8,128)(2,1)S(1)}, bf16[2,64,2048]{2,1,0:T(8,128)(2,1)S(1)}, bf16[2,64,2048]{2,1,0:T(8,128)(2,1)S(1)}) custom-call(s32[2,16]{1,0:T(2,128)} %bitcast.3, s32[16]{0:T(128)} %cont_len.3, s32[2,6]{1,0:T(2,128)} %bitcast.8, bf16[16,2048]{1,0:T(8,128)(2,1)} %new_ref.3, bf16[80,32,2048]{2,1,0:T(8,128)(2,1)} %refs_2_.1), custom_call_target="tpu_custom_call" | custom-call | tf_op jit(solution)/shard_map/send_slots/pallas_call | solution.py:107
  3.1 2.1 %collective-permute-start = (bf16[2,64,2048]{2,1,0:T(8,128)(2,1)S(1)}, bf16[2,64,2048]{2,1,0:T(8,128)(2,1)S(1)}, u32[]{:S(2)}, u32[]{:S(2)}) collective-permute-start(bf16[2,64,2048]{2,1,0:T(8,128)(2,1)S(1)} %get-tuple-element.14), channel_id=1, source_target_pairs={{0,4},{1,5},{2,6},{3,7},{4,0},{5,1},{6,2},{7,3},{8,12},{9,13},{10,... | collective-permute-start | bytes 1572872 | tf_op jit(solution)/shard_map/ppermute | solution.py:304
  5.2 1.3 %collective-permute-start.2 = (bf16[2,64,2048]{2,1,0:T(8,128)(2,1)S(1)}, bf16[2,64,2048]{2,1,0:T(8,128)(2,1)S(1)}, u32[]{:S(2)}, u32[]{:S(2)}) collective-permute-start(bf16[2,64,2048]{2,1,0:T(8,128)(2,1)S(1)} %get-tuple-element.19), channel_id=1, source_target_pairs={{0,2},{1,3},{2,8},{3,1},{4,6},{5,7},{6,12},{7,5},{8,10},{9,11},{10... | collective-permute-start | bytes 1572872 | tf_op jit(solution)/shard_map/ppermute | solution.py:304
  6.4 1.3 %collective-permute-start.6 = (bf16[2,64,2048]{2,1,0:T(8,128)(2,1)S(1)}, bf16[2,64,2048]{2,1,0:T(8,128)(2,1)S(1)}, u32[]{:S(2)}, u32[]{:S(2)}) collective-permute-start(bf16[2,64,2048]{2,1,0:T(8,128)(2,1)S(1)} %get-tuple-element.22), channel_id=1, source_target_pairs={{0,8},{2,10},{4,12},{6,14},{8,16},{10,18},{12,20},{14,22},{16,24},... | collective-permute-start | bytes 1572872 | tf_op jit(solution)/shard_map/ppermute | solution.py:29
  7.8 0.0 copy-done
  7.8 0.0 copy-done.4
  7.8 5.7 %attention.2.refs_0_ = f32[16,2048]{1,0:T(8,128)S(1)} custom-call(s32[2,24]{1,0:T(2,128)S(1)} %copy-done.9, s32[2]{0:T(128)S(1)} %copy-done.10, s32[16]{0:T(128)S(1)} %copy-done.11, s32[2,16]{1,0:T(2,128)S(1)} %bitcast.5, s32[16]{0:T(128)S(1)} %copy-done.6, f32[4]{0:T(128)S(1)} %copy-done.12, bf16[16,1024]{1,0:T(8,128)(2,1)S(1)} %copy-done.2, ...), custom_call_target="tpu_custom_call" | custom-call | flops 201326592 | bytes 7340032 | tf_op jit(solution)/shard_map/attention/pallas_call | solution.py:224
  13.5 0.0 copy-start.1
  13.5 0.0 copy-start.5
  13.5 0.0 copy-start.7
  13.6 2.0 %send_slots.3 = bf16[2,64,2048]{2,1,0:T(8,128)(2,1)S(1)} custom-call(s32[2,16]{1,0:T(2,128)} %bitcast.4, s32[16]{0:T(128)} %cont_len.3, s32[2,6]{1,0:T(2,128)} %bitcast.9, bf16[16,2048]{1,0:T(8,128)(2,1)} %new_ref.3, bf16[80,32,2048]{2,1,0:T(8,128)(2,1)} %refs_2_.1), custom_call_target="tpu_custom_call" | custom-call | tf_op jit(solution)/shard_map/send_slots/pallas_call | solution.py:107
  15.6 0.0 copy-start.3
  15.6 0.0 copy-start.8
  15.6 1.2 %collective-permute-done.refs_0_ = bf16[2,64,2048]{2,1,0:T(8,128)(2,1)S(1)} collective-permute-done((bf16[2,64,2048]{2,1,0:T(8,128)(2,1)S(1)}, bf16[2,64,2048]{2,1,0:T(8,128)(2,1)S(1)}, u32[]{:S(2)}, u32[]{:S(2)}) %collective-permute-start) | collective-permute-done | bytes 524320 | tf_op jit(solution)/shard_map/ppermute | solution.py:304
  16.8 1.2 %collective-permute-start.5 = (bf16[2,64,2048]{2,1,0:T(8,128)(2,1)S(1)}, bf16[2,64,2048]{2,1,0:T(8,128)(2,1)S(1)}, u32[]{:S(2)}, u32[]{:S(2)}) collective-permute-start(bf16[2,64,2048]{2,1,0:T(8,128)(2,1)S(1)} %collective-permute-done.refs_0_), channel_id=1, source_target_pairs={{0,8},{1,9},{2,10},{3,11},{4,5},{5,4},{6,7},{7,6},{8,16},{9,17},{1... | collective-permute-start | bytes 1572872 | tf_op jit(solution)/shard_map/ppermute | solution.py:304
  18.0 2.4 %collective-permute-start.4 = (bf16[2,64,2048]{2,1,0:T(8,128)(2,1)S(1)}, bf16[2,64,2048]{2,1,0:T(8,128)(2,1)S(1)}, u32[]{:S(2)}, u32[]{:S(2)}) collective-permute-start(bf16[2,64,2048]{2,1,0:T(8,128)(2,1)S(1)} %send_slots.3), channel_id=1, source_target_pairs={{0,6},{1,7},{2,4},{3,5},{4,10},{5,11},{6,8},{7,9},{8,14},{9,15},{1... | collective-permute-start | bytes 1572872 | tf_op jit(solution)/shard_map/ppermute | solution.py:304
  20.5 0.0 collective-permute-done.2.refs_2_
  20.5 3.2 %collective-permute-start.3 = (bf16[2,64,2048]{2,1,0:T(8,128)(2,1)S(1)}, bf16[2,64,2048]{2,1,0:T(8,128)(2,1)S(1)}, u32[]{:S(2)}, u32[]{:S(2)}) collective-permute-start(bf16[2,64,2048]{2,1,0:T(8,128)(2,1)S(1)} %collective-permute-done.2.refs_2_), channel_id=1, source_target_pairs={{1,9},{5,13},{9,17},{13,21},{17,25},{21,29},{25,1},{29,5}} | collective-permute-start | bytes 1572872 | tf_op jit(solution)/shard_map/ppermute | solution.py:304
  23.7 5.7 %attention.3.refs_0_ = bf16[16,2048]{1,0:T(8,128)(2,1)S(1)} custom-call(s32[2,24]{1,0:T(2,128)S(1)} %copy-done.9, s32[2]{0:T(128)S(1)} %copy-done.10, s32[16]{0:T(128)S(1)} %copy-done.11, s32[2,16]{1,0:T(2,128)S(1)} %bitcast.6, s32[16]{0:T(128)S(1)} %copy-done.7, f32[4]{0:T(128)S(1)} %copy-done.12, bf16[16,1024]{1,0:T(8,128)(2,1)S(1)} %copy-done.2, ...), custom_call_target="tpu_custom_call" | custom-call | flops 201326592 | bytes 7340032 | tf_op jit(solution)/shard_map/attention/pallas_call | solution.py:224
  29.5 0.1 collective-permute-start.1
  29.5 1.2 %collective-permute-done.1.refs_1_ = bf16[16,2048]{1,0:T(8,128)(2,1)S(1)} collective-permute-done((bf16[16,2048]{1,0:T(8,128)(2,1)S(1)}, bf16[16,2048]{1,0:T(8,128)(2,1)S(1)}, u32[]{:S(2)}, u32[]{:S(2)}) %collective-permute-start.1) | collective-permute-done | bytes 65568 | tf_op jit(solution)/shard_map/ppermute | solution.py:29
  30.8 0.8 %finish.1 = (bf16[16,2048]{1,0:T(8,128)(2,1)}, bf16[16,2048]{1,0:T(8,128)(2,1)}) custom-call(bf16[16,2048]{1,0:T(8,128)(2,1)S(1)} %copy-done.3, f32[1,2048]{1,0:T(1,128)S(1)} %bitcast.7, bf16[16,2048]{1,0:T(8,128)(2,1)S(1)} %attention.3.refs_0_, bf16[16,2048]{1,0:T(8,128)(2,1)S(1)} %collective-permute-done.1.refs_1_), custom_call_target="tpu_custom_call" | custom-call | tf_op jit(solution)/shard_map/finish/pallas_call | solution.py:258
  31.5 0.0 collective-permute-done.6.refs_3_
  31.5 1.1 %collective-permute-done.5.refs_1_ = bf16[2,64,2048]{2,1,0:T(8,128)(2,1)S(1)} collective-permute-done((bf16[2,64,2048]{2,1,0:T(8,128)(2,1)S(1)}, bf16[2,64,2048]{2,1,0:T(8,128)(2,1)S(1)}, u32[]{:S(2)}, u32[]{:S(2)}) %collective-permute-start.5) | collective-permute-done | bytes 524320 | tf_op jit(solution)/shard_map/ppermute | solution.py:304
  32.6 1.0 %arrive.2.refs_2_ = bf16[8,64,2048]{2,1,0:T(8,128)(2,1)} custom-call(bf16[2,64,2048]{2,1,0:T(8,128)(2,1)S(1)} %collective-permute-done.refs_0_, bf16[2,64,2048]{2,1,0:T(8,128)(2,1)S(1)} %collective-permute-done.5.refs_1_, bf16[2,64,2048]{2,1,0:T(8,128)(2,1)S(1)} %collective-permute-done.2.refs_2_, bf16[2,64,2048]{2,1,0:T(8,128)(2,1)S(1)} %collective-permute-done.6.refs_3_), custom_call_target="tpu_custom_call" | custom-call | tf_op jit(solution)/shard_map/arrive/pallas_call | solution.py:283
  33.7 2.4 %collective-permute-done.4.refs_1_ = bf16[2,64,2048]{2,1,0:T(8,128)(2,1)S(1)} collective-permute-done((bf16[2,64,2048]{2,1,0:T(8,128)(2,1)S(1)}, bf16[2,64,2048]{2,1,0:T(8,128)(2,1)S(1)}, u32[]{:S(2)}, u32[]{:S(2)}) %collective-permute-start.4) | collective-permute-done | bytes 524320 | tf_op jit(solution)/shard_map/ppermute | solution.py:304
  36.0 2.9 %collective-permute-done.3.refs_0_ = bf16[2,64,2048]{2,1,0:T(8,128)(2,1)S(1)} collective-permute-done((bf16[2,64,2048]{2,1,0:T(8,128)(2,1)S(1)}, bf16[2,64,2048]{2,1,0:T(8,128)(2,1)S(1)}, u32[]{:S(2)}, u32[]{:S(2)}) %collective-permute-start.3) | collective-permute-done | bytes 524320 | tf_op jit(solution)/shard_map/ppermute | solution.py:304
  38.9 1.0 %arrive.3 = bf16[8,64,2048]{2,1,0:T(8,128)(2,1)} custom-call(bf16[2,64,2048]{2,1,0:T(8,128)(2,1)S(1)} %collective-permute-done.3.refs_0_, bf16[2,64,2048]{2,1,0:T(8,128)(2,1)S(1)} %collective-permute-done.4.refs_1_, bf16[8,64,2048]{2,1,0:T(8,128)(2,1)} %arrive.2.refs_2_), custom_call_target="tpu_custom_call", output_to_operand_aliasing={{}: (2, {})} | custom-call | tf_op jit(solution)/shard_map/arrive/pallas_call | solution.py:283
  (15 shorter events, 0.0 us)
Async XLA Ops:
  0.6 7.1 %copy-start = (bf16[16,2048]{1,0:T(8,128)(2,1)S(1)}, bf16[16,2048]{1,0:T(8,128)(2,1)}, u32[]{:S(2)}) copy-start(bf16[16,2048]{1,0:T(8,128)(2,1)} %new_ref.3) | copy-start | bytes 196612
  0.6 7.1 %copy-start.2 = (bf16[16,1024]{1,0:T(8,128)(2,1)S(1)}, bf16[16,1024]{1,0:T(8,128)(2,1)}, u32[]{:S(2)}) copy-start(bf16[16,1024]{1,0:T(8,128)(2,1)} %query.3) | copy-start | bytes 98308
  0.7 7.1 %copy-start.4 = (s32[16,2]{0,1:T(2,128)S(1)}, s32[16,2]{0,1:T(2,128)}, u32[]{:S(2)}) copy-start(s32[16,2]{0,1:T(2,128)} %param.20) | copy-start | bytes 388
  0.7 7.1 %copy-start.6 = (s32[16]{0:T(128)S(1)}, s32[16]{0:T(128)}, u32[]{:S(2)}) copy-start(s32[16]{0:T(128)} %cont_len.3) | copy-start | bytes 196
  0.7 7.1 %copy-start.9 = (s32[2,24]{1,0:T(2,128)S(1)}, s32[2,24]{1,0:T(2,128)}, u32[]{:S(2)}) copy-start(s32[2,24]{1,0:T(2,128)} %prompt_table.3) | copy-start | bytes 580
  0.7 7.1 %copy-start.10 = (s32[2]{0:T(128)S(1)}, s32[2]{0:T(128)}, u32[]{:S(2)}) copy-start(s32[2]{0:T(128)} %prompt_len.3) | copy-start | bytes 28
  0.7 7.1 %copy-start.11 = (s32[16]{0:T(128)S(1)}, s32[16]{0:T(128)}, u32[]{:S(2)}) copy-start(s32[16]{0:T(128)} %req_group.3) | copy-start | bytes 196
  0.7 7.1 %copy-start.12 = (f32[4]{0:T(128)S(1)}, f32[4]{0:T(128)}, u32[]{:S(2)}) copy-start(f32[4]{0:T(128)} %lam.3) | copy-start | bytes 52
  3.1 13.7 %collective-permute-start = (bf16[2,64,2048]{2,1,0:T(8,128)(2,1)S(1)}, bf16[2,64,2048]{2,1,0:T(8,128)(2,1)S(1)}, u32[]{:S(2)}, u32[]{:S(2)}) collective-permute-start(bf16[2,64,2048]{2,1,0:T(8,128)(2,1)S(1)} %get-tuple-element.14), channel_id=1, source_target_pairs={{0,4},{1,5},{2,6},{3,7},{4,0},{5,1},{6,2},{7,3},{8,12},{9,13},{10,... | collective-permute-start | bytes 1572872 | tf_op jit(solution)/shard_map/ppermute | solution.py:304
  5.2 15.3 %collective-permute-start.2 = (bf16[2,64,2048]{2,1,0:T(8,128)(2,1)S(1)}, bf16[2,64,2048]{2,1,0:T(8,128)(2,1)S(1)}, u32[]{:S(2)}, u32[]{:S(2)}) collective-permute-start(bf16[2,64,2048]{2,1,0:T(8,128)(2,1)S(1)} %get-tuple-element.19), channel_id=1, source_target_pairs={{0,2},{1,3},{2,8},{3,1},{4,6},{5,7},{6,12},{7,5},{8,10},{9,11},{10... | collective-permute-start | bytes 1572872 | tf_op jit(solution)/shard_map/ppermute | solution.py:304
  6.4 25.1 %collective-permute-start.6 = (bf16[2,64,2048]{2,1,0:T(8,128)(2,1)S(1)}, bf16[2,64,2048]{2,1,0:T(8,128)(2,1)S(1)}, u32[]{:S(2)}, u32[]{:S(2)}) collective-permute-start(bf16[2,64,2048]{2,1,0:T(8,128)(2,1)S(1)} %get-tuple-element.22), channel_id=1, source_target_pairs={{0,8},{2,10},{4,12},{6,14},{8,16},{10,18},{12,20},{14,22},{16,24},... | collective-permute-start | bytes 1572872 | tf_op jit(solution)/shard_map/ppermute | solution.py:29
  13.5 10.2 %copy-start.1 = (bf16[16,2048]{1,0:T(8,128)(2,1)S(1)}, bf16[16,2048]{1,0:T(8,128)(2,1)}, u32[]{:S(2)}) copy-start(bf16[16,2048]{1,0:T(8,128)(2,1)} %new_ref.3) | copy-start | bytes 196612
  13.5 10.2 %copy-start.5 = (s32[16,2]{0,1:T(2,128)S(1)}, s32[16,2]{0,1:T(2,128)}, u32[]{:S(2)}) copy-start(s32[16,2]{0,1:T(2,128)} %param.20) | copy-start | bytes 388
  13.5 10.2 %copy-start.7 = (s32[16]{0:T(128)S(1)}, s32[16]{0:T(128)}, u32[]{:S(2)}) copy-start(s32[16]{0:T(128)} %cont_len.3) | copy-start | bytes 196
  15.6 15.2 %copy-start.3 = (bf16[16,2048]{1,0:T(8,128)(2,1)S(1)}, bf16[16,2048]{1,0:T(8,128)(2,1)}, u32[]{:S(2)}) copy-start(bf16[16,2048]{1,0:T(8,128)(2,1)} %hidden.1) | copy-start | bytes 196612
  15.6 15.2 %copy-start.8 = (f32[2048]{0:T(1024)S(1)}, f32[2048]{0:T(1024)}, u32[]{:S(2)}) copy-start(f32[2048]{0:T(1024)} %param.25) | copy-start | bytes 24580
  16.8 15.8 %collective-permute-start.5 = (bf16[2,64,2048]{2,1,0:T(8,128)(2,1)S(1)}, bf16[2,64,2048]{2,1,0:T(8,128)(2,1)S(1)}, u32[]{:S(2)}, u32[]{:S(2)}) collective-permute-start(bf16[2,64,2048]{2,1,0:T(8,128)(2,1)S(1)} %collective-permute-done.refs_0_), channel_id=1, source_target_pairs={{0,8},{1,9},{2,10},{3,11},{4,5},{5,4},{6,7},{7,6},{8,16},{9,17},{1... | collective-permute-start | bytes 1572872 | tf_op jit(solution)/shard_map/ppermute | solution.py:304
  18.0 18.0 %collective-permute-start.4 = (bf16[2,64,2048]{2,1,0:T(8,128)(2,1)S(1)}, bf16[2,64,2048]{2,1,0:T(8,128)(2,1)S(1)}, u32[]{:S(2)}, u32[]{:S(2)}) collective-permute-start(bf16[2,64,2048]{2,1,0:T(8,128)(2,1)S(1)} %send_slots.3), channel_id=1, source_target_pairs={{0,6},{1,7},{2,4},{3,5},{4,10},{5,11},{6,8},{7,9},{8,14},{9,15},{1... | collective-permute-start | bytes 1572872 | tf_op jit(solution)/shard_map/ppermute | solution.py:304
  20.5 18.4 %collective-permute-start.3 = (bf16[2,64,2048]{2,1,0:T(8,128)(2,1)S(1)}, bf16[2,64,2048]{2,1,0:T(8,128)(2,1)S(1)}, u32[]{:S(2)}, u32[]{:S(2)}) collective-permute-start(bf16[2,64,2048]{2,1,0:T(8,128)(2,1)S(1)} %collective-permute-done.2.refs_2_), channel_id=1, source_target_pairs={{1,9},{5,13},{9,17},{13,21},{17,25},{21,29},{25,1},{29,5}} | collective-permute-start | bytes 1572872 | tf_op jit(solution)/shard_map/ppermute | solution.py:304
  29.5 1.3 %collective-permute-start.1 = (bf16[16,2048]{1,0:T(8,128)(2,1)S(1)}, bf16[16,2048]{1,0:T(8,128)(2,1)S(1)}, u32[]{:S(2)}, u32[]{:S(2)}) collective-permute-start(bf16[16,2048]{1,0:T(8,128)(2,1)S(1)} %attention.3.refs_0_), channel_id=1, source_target_pairs={{0,1},{1,0},{2,3},{3,2},{4,5},{5,4},{6,7},{7,6},{8,9},{9,8},{10,11... | collective-permute-start | bytes 196616 | tf_op jit(solution)/shard_map/ppermute | solution.py:29

commit v3 on v0

--- a/solution.py
+++ b/solution.py
@@ -310,7 +310,7 @@
 def route_early(s, odd):
     if s % 2 == 0:
         return s + 1
-    return turn(s, 3) if odd else s + 3
+    return turn(s, 3) if odd == (s % MIG_REACH == 1) else s + 3
 
 
 def route_late(s, odd):
@@ -322,7 +322,7 @@
 
 
 def lift_early(s, odd):
-    return s + MIG_REACH if odd and s % 2 == 0 else None
+    return s + MIG_REACH if s % 2 == 0 and odd == (s % MIG_REACH == 0) else None
 
 
 def choose_straight():
@@ -338,12 +338,12 @@
 
 def choose_sooner():
     col, odd, even, odd_core = where_am_i()
-    return [(0, 2, odd), (2, 0, col >= 2), (2, 1, col < 2), (4, 2, even & jnp.logical_not(odd_core)), (6, 3, True)]
+    return [(0, 2, odd), (2, 0, col >= 2), (2, 1, col < 2), (4, 2, even & (odd_core != (col == 0))), (6, 3, True)]
 
 
 def choose_later():
     col, odd, even, odd_core = where_am_i()
-    return [(0, 1, even), (4, 1, odd), (4, 0, even & odd_core)]
+    return [(0, 1, even), (4, 1, odd), (4, 0, even & (odd_core == (col == 0)))]
 
 
 def can_relay():

time: 40.5 us -> 40.5 us (level)
  no operation moved by 1% of the time
where the time goes in v3:
time: 40.5 us; the launch traced here: 39.8 us
  Pallas kernels  18.5 us (46%)
  starting transfers between devices  11.3 us (28%)
  waiting for transfers between devices  9.07 us (22%)
  between operations  0.86 us (2%)
    pallas_call x2, Pallas kernels, attention(): pl.pallas_call(functools.partial(attention_kernel, low), out_shape=jax.Sh...  11.4 us
    ppermute x5, starting transfers between devices, routed(): return lax.ppermute(value, ('req', 'tp'), pairs)  9.92 us
    ppermute x5, waiting for transfers between devices, routed(): return lax.ppermute(value, ('req', 'tp'), pairs)  7.83 us
    pallas_call x2, Pallas kernels, send_slots(): pl.pallas_call(functools.partial(send_kernel, offsets), out_shape=[jax.Sh...  4.3 us
    pallas_call x2, Pallas kernels, arrive(): pl.pallas_call(functools.partial(gather_kernel, choose, len(parts)), out_...  2.07 us
    ppermute x2, starting transfers between devices, shifted(): return lax.ppermute(value, axis, pairs)  1.37 us
    ppermute x2, waiting for transfers between devices, shifted(): return lax.ppermute(value, axis, pairs)  1.24 us
  transfers between devices with their start and end apart: 7, of which 5 were waited for; matrix products, arithmetic and copies ran while one was open for 0% of the time, Pallas kernels for 38%

profile of v3, /device:TPU:1, one launch (start us, length us, event | category | flops | bytes accessed | tf_op | source)
XLA Modules:
  0.0 39.8 jit_solution(10519909677517616647)
XLA Ops:
  0.6 0.0 copy-start
  0.7 0.0 copy-start.4
  0.7 0.0 copy-start.6
  0.7 0.0 copy-start.9
  0.7 0.0 copy-start.10
  0.7 0.0 copy-start.11
  0.7 2.4 %send_slots.2 = (bf16[2,64,2048]{2,1,0:T(8,128)(2,1)S(1)}, bf16[2,64,2048]{2,1,0:T(8,128)(2,1)S(1)}, bf16[2,64,2048]{2,1,0:T(8,128)(2,1)S(1)}) custom-call(s32[2,16]{1,0:T(2,128)} %bitcast.3, s32[16]{0:T(128)} %cont_len.3, s32[2,6]{1,0:T(2,128)} %bitcast.8, bf16[16,2048]{1,0:T(8,128)(2,1)} %new_ref.3, bf16[80,32,2048]{2,1,0:T(8,128)(2,1)} %refs_2_.1), custom_call_target="tpu_custom_call" | custom-call | tf_op jit(solution)/shard_map/send_slots/pallas_call | solution.py:106
  3.1 2.2 %collective-permute-start = (bf16[2,64,2048]{2,1,0:T(8,128)(2,1)S(1)}, bf16[2,64,2048]{2,1,0:T(8,128)(2,1)S(1)}, u32[]{:S(2)}, u32[]{:S(2)}) collective-permute-start(bf16[2,64,2048]{2,1,0:T(8,128)(2,1)S(1)} %get-tuple-element.14), channel_id=1, source_target_pairs={{0,4},{1,5},{2,6},{3,7},{4,0},{5,1},{6,2},{7,3},{8,12},{9,13},{10,... | collective-permute-start | bytes 1572872 | tf_op jit(solution)/shard_map/ppermute | solution.py:303
  5.3 1.1 %collective-permute-start.2 = (bf16[2,64,2048]{2,1,0:T(8,128)(2,1)S(1)}, bf16[2,64,2048]{2,1,0:T(8,128)(2,1)S(1)}, u32[]{:S(2)}, u32[]{:S(2)}) collective-permute-start(bf16[2,64,2048]{2,1,0:T(8,128)(2,1)S(1)} %get-tuple-element.19), channel_id=1, source_target_pairs={{0,2},{1,3},{2,8},{3,1},{4,6},{5,7},{6,4},{7,13},{8,10},{9,11},{10... | collective-permute-start | bytes 1572872 | tf_op jit(solution)/shard_map/ppermute | solution.py:303
  6.3 1.3 %collective-permute-start.6 = (bf16[2,64,2048]{2,1,0:T(8,128)(2,1)S(1)}, bf16[2,64,2048]{2,1,0:T(8,128)(2,1)S(1)}, u32[]{:S(2)}, u32[]{:S(2)}) collective-permute-start(bf16[2,64,2048]{2,1,0:T(8,128)(2,1)S(1)} %get-tuple-element.22), channel_id=1, source_target_pairs={{0,8},{2,10},{4,12},{6,14},{8,16},{10,18},{12,20},{14,22},{16,24},... | collective-permute-start | bytes 1572872 | tf_op jit(solution)/shard_map/ppermute | solution.py:29
  7.7 5.7 %attention.2.refs_0_ = f32[16,2048]{1,0:T(8,128)S(1)} custom-call(s32[2,24]{1,0:T(2,128)S(1)} %copy-done.9, s32[2]{0:T(128)S(1)} %copy-done.10, s32[16]{0:T(128)S(1)} %copy-done.11, s32[2,16]{1,0:T(2,128)S(1)} %bitcast.5, s32[16]{0:T(128)S(1)} %copy-done.6, f32[4]{0:T(128)S(1)} %copy-done.12, bf16[16,1024]{1,0:T(8,128)(2,1)S(1)} %copy-done.2, ...), custom_call_target="tpu_custom_call" | custom-call | flops 201326592 | bytes 7340032 | tf_op jit(solution)/shard_map/attention/pallas_call | solution.py:223
  13.4 0.0 copy-start.1
  13.4 0.0 copy-start.5
  13.4 0.0 copy-start.7
  13.4 1.9 %send_slots.3 = bf16[2,64,2048]{2,1,0:T(8,128)(2,1)S(1)} custom-call(s32[2,16]{1,0:T(2,128)} %bitcast.4, s32[16]{0:T(128)} %cont_len.3, s32[2,6]{1,0:T(2,128)} %bitcast.9, bf16[16,2048]{1,0:T(8,128)(2,1)} %new_ref.3, bf16[80,32,2048]{2,1,0:T(8,128)(2,1)} %refs_2_.1), custom_call_target="tpu_custom_call" | custom-call | tf_op jit(solution)/shard_map/send_slots/pallas_call | solution.py:106
  15.4 0.0 copy-start.3
  15.4 0.0 copy-start.8
  15.4 1.5 %collective-permute-done.refs_0_ = bf16[2,64,2048]{2,1,0:T(8,128)(2,1)S(1)} collective-permute-done((bf16[2,64,2048]{2,1,0:T(8,128)(2,1)S(1)}, bf16[2,64,2048]{2,1,0:T(8,128)(2,1)S(1)}, u32[]{:S(2)}, u32[]{:S(2)}) %collective-permute-start) | collective-permute-done | bytes 524320 | tf_op jit(solution)/shard_map/ppermute | solution.py:303
  16.9 1.0 %collective-permute-start.5 = (bf16[2,64,2048]{2,1,0:T(8,128)(2,1)S(1)}, bf16[2,64,2048]{2,1,0:T(8,128)(2,1)S(1)}, u32[]{:S(2)}, u32[]{:S(2)}) collective-permute-start(bf16[2,64,2048]{2,1,0:T(8,128)(2,1)S(1)} %collective-permute-done.refs_0_), channel_id=1, source_target_pairs={{0,8},{1,9},{2,10},{3,11},{4,5},{5,4},{6,7},{7,6},{8,16},{9,17},{1... | collective-permute-start | bytes 1572872 | tf_op jit(solution)/shard_map/ppermute | solution.py:303
  18.0 2.4 %collective-permute-start.4 = (bf16[2,64,2048]{2,1,0:T(8,128)(2,1)S(1)}, bf16[2,64,2048]{2,1,0:T(8,128)(2,1)S(1)}, u32[]{:S(2)}, u32[]{:S(2)}) collective-permute-start(bf16[2,64,2048]{2,1,0:T(8,128)(2,1)S(1)} %send_slots.3), channel_id=1, source_target_pairs={{0,6},{1,7},{2,4},{3,5},{4,10},{5,11},{6,8},{7,9},{8,14},{9,15},{1... | collective-permute-start | bytes 1572872 | tf_op jit(solution)/shard_map/ppermute | solution.py:303
  20.4 0.0 collective-permute-done.2.refs_2_
  20.4 3.2 %collective-permute-start.3 = (bf16[2,64,2048]{2,1,0:T(8,128)(2,1)S(1)}, bf16[2,64,2048]{2,1,0:T(8,128)(2,1)S(1)}, u32[]{:S(2)}, u32[]{:S(2)}) collective-permute-start(bf16[2,64,2048]{2,1,0:T(8,128)(2,1)S(1)} %collective-permute-done.2.refs_2_), channel_id=1, source_target_pairs={{1,9},{4,12},{9,17},{12,20},{17,25},{20,28},{25,1},{28,4}} | collective-permute-start | bytes 1572872 | tf_op jit(solution)/shard_map/ppermute | solution.py:303
  23.6 5.7 %attention.3.refs_0_ = bf16[16,2048]{1,0:T(8,128)(2,1)S(1)} custom-call(s32[2,24]{1,0:T(2,128)S(1)} %copy-done.9, s32[2]{0:T(128)S(1)} %copy-done.10, s32[16]{0:T(128)S(1)} %copy-done.11, s32[2,16]{1,0:T(2,128)S(1)} %bitcast.6, s32[16]{0:T(128)S(1)} %copy-done.7, f32[4]{0:T(128)S(1)} %copy-done.12, bf16[16,1024]{1,0:T(8,128)(2,1)S(1)} %copy-done.2, ...), custom_call_target="tpu_custom_call" | custom-call | flops 201326592 | bytes 7340032 | tf_op jit(solution)/shard_map/attention/pallas_call | solution.py:223
  29.4 0.1 collective-permute-start.1
  29.4 1.2 %collective-permute-done.1.refs_1_ = bf16[16,2048]{1,0:T(8,128)(2,1)S(1)} collective-permute-done((bf16[16,2048]{1,0:T(8,128)(2,1)S(1)}, bf16[16,2048]{1,0:T(8,128)(2,1)S(1)}, u32[]{:S(2)}, u32[]{:S(2)}) %collective-permute-start.1) | collective-permute-done | bytes 65568 | tf_op jit(solution)/shard_map/ppermute | solution.py:29
  30.7 0.8 %finish.1 = (bf16[16,2048]{1,0:T(8,128)(2,1)}, bf16[16,2048]{1,0:T(8,128)(2,1)}) custom-call(bf16[16,2048]{1,0:T(8,128)(2,1)S(1)} %copy-done.3, f32[1,2048]{1,0:T(1,128)S(1)} %bitcast.7, bf16[16,2048]{1,0:T(8,128)(2,1)S(1)} %attention.3.refs_0_, bf16[16,2048]{1,0:T(8,128)(2,1)S(1)} %collective-permute-done.1.refs_1_), custom_call_target="tpu_custom_call" | custom-call | tf_op jit(solution)/shard_map/finish/pallas_call | solution.py:257
  31.4 0.0 collective-permute-done.6.refs_3_
  31.4 1.1 %collective-permute-done.5.refs_1_ = bf16[2,64,2048]{2,1,0:T(8,128)(2,1)S(1)} collective-permute-done((bf16[2,64,2048]{2,1,0:T(8,128)(2,1)S(1)}, bf16[2,64,2048]{2,1,0:T(8,128)(2,1)S(1)}, u32[]{:S(2)}, u32[]{:S(2)}) %collective-permute-start.5) | collective-permute-done | bytes 524320 | tf_op jit(solution)/shard_map/ppermute | solution.py:303
  32.5 1.0 %arrive.2.refs_2_ = bf16[8,64,2048]{2,1,0:T(8,128)(2,1)} custom-call(bf16[2,64,2048]{2,1,0:T(8,128)(2,1)S(1)} %collective-permute-done.refs_0_, bf16[2,64,2048]{2,1,0:T(8,128)(2,1)S(1)} %collective-permute-done.5.refs_1_, bf16[2,64,2048]{2,1,0:T(8,128)(2,1)S(1)} %collective-permute-done.2.refs_2_, bf16[2,64,2048]{2,1,0:T(8,128)(2,1)S(1)} %collective-permute-done.6.refs_3_), custom_call_target="tpu_custom_call" | custom-call | tf_op jit(solution)/shard_map/arrive/pallas_call | solution.py:282
  33.6 4.9 %collective-permute-done.4.refs_1_ = bf16[2,64,2048]{2,1,0:T(8,128)(2,1)S(1)} collective-permute-done((bf16[2,64,2048]{2,1,0:T(8,128)(2,1)S(1)}, bf16[2,64,2048]{2,1,0:T(8,128)(2,1)S(1)}, u32[]{:S(2)}, u32[]{:S(2)}) %collective-permute-start.4) | collective-permute-done | bytes 524320 | tf_op jit(solution)/shard_map/ppermute | solution.py:303
  38.5 0.3 collective-permute-done.3.refs_0_
  38.8 1.0 %arrive.3 = bf16[8,64,2048]{2,1,0:T(8,128)(2,1)} custom-call(bf16[2,64,2048]{2,1,0:T(8,128)(2,1)S(1)} %collective-permute-done.3.refs_0_, bf16[2,64,2048]{2,1,0:T(8,128)(2,1)S(1)} %collective-permute-done.4.refs_1_, bf16[8,64,2048]{2,1,0:T(8,128)(2,1)} %arrive.2.refs_2_), custom_call_target="tpu_custom_call", output_to_operand_aliasing={{}: (2, {})} | custom-call | tf_op jit(solution)/shard_map/arrive/pallas_call | solution.py:282
  (15 shorter events, 0.0 us)
Async XLA Ops:
  0.6 7.0 %copy-start = (bf16[16,2048]{1,0:T(8,128)(2,1)S(1)}, bf16[16,2048]{1,0:T(8,128)(2,1)}, u32[]{:S(2)}) copy-start(bf16[16,2048]{1,0:T(8,128)(2,1)} %new_ref.3) | copy-start | bytes 196612
  0.6 7.0 %copy-start.2 = (bf16[16,1024]{1,0:T(8,128)(2,1)S(1)}, bf16[16,1024]{1,0:T(8,128)(2,1)}, u32[]{:S(2)}) copy-start(bf16[16,1024]{1,0:T(8,128)(2,1)} %query.3) | copy-start | bytes 98308
  0.7 7.0 %copy-start.4 = (s32[16,2]{0,1:T(2,128)S(1)}, s32[16,2]{0,1:T(2,128)}, u32[]{:S(2)}) copy-start(s32[16,2]{0,1:T(2,128)} %param.20) | copy-start | bytes 388
  0.7 7.0 %copy-start.6 = (s32[16]{0:T(128)S(1)}, s32[16]{0:T(128)}, u32[]{:S(2)}) copy-start(s32[16]{0:T(128)} %cont_len.3) | copy-start | bytes 196
  0.7 7.0 %copy-start.9 = (s32[2,24]{1,0:T(2,128)S(1)}, s32[2,24]{1,0:T(2,128)}, u32[]{:S(2)}) copy-start(s32[2,24]{1,0:T(2,128)} %prompt_table.3) | copy-start | bytes 580
  0.7 7.0 %copy-start.10 = (s32[2]{0:T(128)S(1)}, s32[2]{0:T(128)}, u32[]{:S(2)}) copy-start(s32[2]{0:T(128)} %prompt_len.3) | copy-start | bytes 28
  0.7 7.0 %copy-start.11 = (s32[16]{0:T(128)S(1)}, s32[16]{0:T(128)}, u32[]{:S(2)}) copy-start(s32[16]{0:T(128)} %req_group.3) | copy-start | bytes 196
  0.7 7.0 %copy-start.12 = (f32[4]{0:T(128)S(1)}, f32[4]{0:T(128)}, u32[]{:S(2)}) copy-start(f32[4]{0:T(128)} %lam.3) | copy-start | bytes 52
  3.1 13.8 %collective-permute-start = (bf16[2,64,2048]{2,1,0:T(8,128)(2,1)S(1)}, bf16[2,64,2048]{2,1,0:T(8,128)(2,1)S(1)}, u32[]{:S(2)}, u32[]{:S(2)}) collective-permute-start(bf16[2,64,2048]{2,1,0:T(8,128)(2,1)S(1)} %get-tuple-element.14), channel_id=1, source_target_pairs={{0,4},{1,5},{2,6},{3,7},{4,0},{5,1},{6,2},{7,3},{8,12},{9,13},{10,... | collective-permute-start | bytes 1572872 | tf_op jit(solution)/shard_map/ppermute | solution.py:303
  5.3 15.1 %collective-permute-start.2 = (bf16[2,64,2048]{2,1,0:T(8,128)(2,1)S(1)}, bf16[2,64,2048]{2,1,0:T(8,128)(2,1)S(1)}, u32[]{:S(2)}, u32[]{:S(2)}) collective-permute-start(bf16[2,64,2048]{2,1,0:T(8,128)(2,1)S(1)} %get-tuple-element.19), channel_id=1, source_target_pairs={{0,2},{1,3},{2,8},{3,1},{4,6},{5,7},{6,4},{7,13},{8,10},{9,11},{10... | collective-permute-start | bytes 1572872 | tf_op jit(solution)/shard_map/ppermute | solution.py:303
  6.3 25.1 %collective-permute-start.6 = (bf16[2,64,2048]{2,1,0:T(8,128)(2,1)S(1)}, bf16[2,64,2048]{2,1,0:T(8,128)(2,1)S(1)}, u32[]{:S(2)}, u32[]{:S(2)}) collective-permute-start(bf16[2,64,2048]{2,1,0:T(8,128)(2,1)S(1)} %get-tuple-element.22), channel_id=1, source_target_pairs={{0,8},{2,10},{4,12},{6,14},{8,16},{10,18},{12,20},{14,22},{16,24},... | collective-permute-start | bytes 1572872 | tf_op jit(solution)/shard_map/ppermute | solution.py:29
  13.4 10.2 %copy-start.1 = (bf16[16,2048]{1,0:T(8,128)(2,1)S(1)}, bf16[16,2048]{1,0:T(8,128)(2,1)}, u32[]{:S(2)}) copy-start(bf16[16,2048]{1,0:T(8,128)(2,1)} %new_ref.3) | copy-start | bytes 196612
  13.4 10.2 %copy-start.5 = (s32[16,2]{0,1:T(2,128)S(1)}, s32[16,2]{0,1:T(2,128)}, u32[]{:S(2)}) copy-start(s32[16,2]{0,1:T(2,128)} %param.20) | copy-start | bytes 388
  13.4 10.2 %copy-start.7 = (s32[16]{0:T(128)S(1)}, s32[16]{0:T(128)}, u32[]{:S(2)}) copy-start(s32[16]{0:T(128)} %cont_len.3) | copy-start | bytes 196
  15.4 15.3 %copy-start.3 = (bf16[16,2048]{1,0:T(8,128)(2,1)S(1)}, bf16[16,2048]{1,0:T(8,128)(2,1)}, u32[]{:S(2)}) copy-start(bf16[16,2048]{1,0:T(8,128)(2,1)} %hidden.1) | copy-start | bytes 196612
  15.4 15.3 %copy-start.8 = (f32[2048]{0:T(1024)S(1)}, f32[2048]{0:T(1024)}, u32[]{:S(2)}) copy-start(f32[2048]{0:T(1024)} %param.25) | copy-start | bytes 24580
  16.9 15.6 %collective-permute-start.5 = (bf16[2,64,2048]{2,1,0:T(8,128)(2,1)S(1)}, bf16[2,64,2048]{2,1,0:T(8,128)(2,1)S(1)}, u32[]{:S(2)}, u32[]{:S(2)}) collective-permute-start(bf16[2,64,2048]{2,1,0:T(8,128)(2,1)S(1)} %collective-permute-done.refs_0_), channel_id=1, source_target_pairs={{0,8},{1,9},{2,10},{3,11},{4,5},{5,4},{6,7},{7,6},{8,16},{9,17},{1... | collective-permute-start | bytes 1572872 | tf_op jit(solution)/shard_map/ppermute | solution.py:303
  18.0 20.5 %collective-permute-start.4 = (bf16[2,64,2048]{2,1,0:T(8,128)(2,1)S(1)}, bf16[2,64,2048]{2,1,0:T(8,128)(2,1)S(1)}, u32[]{:S(2)}, u32[]{:S(2)}) collective-permute-start(bf16[2,64,2048]{2,1,0:T(8,128)(2,1)S(1)} %send_slots.3), channel_id=1, source_target_pairs={{0,6},{1,7},{2,4},{3,5},{4,10},{5,11},{6,8},{7,9},{8,14},{9,15},{1... | collective-permute-start | bytes 1572872 | tf_op jit(solution)/shard_map/ppermute | solution.py:303
  20.4 18.4 %collective-permute-start.3 = (bf16[2,64,2048]{2,1,0:T(8,128)(2,1)S(1)}, bf16[2,64,2048]{2,1,0:T(8,128)(2,1)S(1)}, u32[]{:S(2)}, u32[]{:S(2)}) collective-permute-start(bf16[2,64,2048]{2,1,0:T(8,128)(2,1)S(1)} %collective-permute-done.2.refs_2_), channel_id=1, source_target_pairs={{1,9},{4,12},{9,17},{12,20},{17,25},{20,28},{25,1},{28,4}} | collective-permute-start | bytes 1572872 | tf_op jit(solution)/shard_map/ppermute | solution.py:303
  29.4 1.3 %collective-permute-start.1 = (bf16[16,2048]{1,0:T(8,128)(2,1)S(1)}, bf16[16,2048]{1,0:T(8,128)(2,1)S(1)}, u32[]{:S(2)}, u32[]{:S(2)}) collective-permute-start(bf16[16,2048]{1,0:T(8,128)(2,1)S(1)} %attention.3.refs_0_), channel_id=1, source_target_pairs={{0,1},{1,0},{2,3},{3,2},{4,5},{5,4},{6,7},{7,6},{8,9},{9,8},{10,11... | collective-permute-start | bytes 196616 | tf_op jit(solution)/shard_map/ppermute | solution.py:29

commit v4 on v3

--- a/solution.py
+++ b/solution.py
@@ -341,9 +341,14 @@
     return [(0, 2, odd), (2, 0, col >= 2), (2, 1, col < 2), (4, 2, even & (odd_core != (col == 0))), (6, 3, True)]
 
 
-def choose_later():
+def choose_late():
     col, odd, even, odd_core = where_am_i()
-    return [(0, 1, even), (4, 1, odd), (4, 0, even & (odd_core == (col == 0)))]
+    return [(0, 0, even), (4, 0, odd)]
+
+
+def choose_last():
+    col, odd, even, odd_core = where_am_i()
+    return [(4, 0, even & (odd_core == (col == 0)))]
 
 
 def can_relay():
@@ -396,7 +401,8 @@
     hidden_out, normed_out = finish(hidden_in, norm_gain, parts)
     if can_relay():
         sooner = arrive((two, two_up, early, four), choose_sooner)
-        arrived = arrive((early_up, late), choose_later, sooner)
+        later = arrive((late,), choose_late, sooner)
+        arrived = arrive((early_up,), choose_last, later)
     return (hidden_out, normed_out, arrived)
 
 

time: 40.5 us -> 40.6 us (level)
  Pallas kernels: 18.5 us -> 19.2 us
  waiting for transfers between devices: 9.07 us -> 8.55 us
    pallas_call x2 -> x3, Pallas kernels: 2.07 us -> 2.78 us  [arrive(): pl.pallas_call(functools.partial(gather_kernel, choose, len(parts)), out_...]
    ppermute x5, waiting for transfers between devices: 7.83 us -> 7.3 us  [routed(): return lax.ppermute(value, ('req', 'tp'), pairs)]
  transfers between devices with their start and end apart: 7 -> 7, of which waited for: 5 -> 4; matrix products, arithmetic and copies ran while one was open for 0% -> 0% of each run, Pallas kernels for 38% -> 40%
where the time goes in v4:
time: 40.6 us; the launch traced here: 40.2 us
  Pallas kernels  19.2 us (47%)
  starting transfers between devices  11.5 us (28%)
  waiting for transfers between devices  8.55 us (21%)
  between operations  0.87 us (2%)
    pallas_call x2, Pallas kernels, attention(): pl.pallas_call(functools.partial(attention_kernel, low), out_shape=jax.Sh...  11.4 us
    ppermute x5, starting transfers between devices, routed(): return lax.ppermute(value, ('req', 'tp'), pairs)  10.1 us
    ppermute x5, waiting for transfers between devices, routed(): return lax.ppermute(value, ('req', 'tp'), pairs)  7.3 us
    pallas_call x2, Pallas kernels, send_slots(): pl.pallas_call(functools.partial(send_kernel, offsets), out_shape=[jax.Sh...  4.29 us
    pallas_call x3, Pallas kernels, arrive(): pl.pallas_call(functools.partial(gather_kernel, choose, len(parts)), out_...  2.78 us
    ppermute x2, starting transfers between devices, shifted(): return lax.ppermute(value, axis, pairs)  1.32 us
    ppermute x2, waiting for transfers between devices, shifted(): return lax.ppermute(value, axis, pairs)  1.24 us
  transfers between devices with their start and end apart: 7, of which 4 were waited for; matrix products, arithmetic and copies ran while one was open for 0% of the time, Pallas kernels for 40%

profile of v4, /device:TPU:1, one launch (start us, length us, event | category | flops | bytes accessed | tf_op | source)
XLA Modules:
  0.0 40.2 jit_solution(1976907261424913458)
XLA Ops:
  0.6 0.0 copy-start
  0.7 0.0 copy-start.4
  0.7 0.0 copy-start.6
  0.7 2.3 %send_slots.2 = (bf16[2,64,2048]{2,1,0:T(8,128)(2,1)S(1)}, bf16[2,64,2048]{2,1,0:T(8,128)(2,1)S(1)}, bf16[2,64,2048]{2,1,0:T(8,128)(2,1)S(1)}) custom-call(s32[2,16]{1,0:T(2,128)} %bitcast.3, s32[16]{0:T(128)} %cont_len.3, s32[2,6]{1,0:T(2,128)} %bitcast.8, bf16[16,2048]{1,0:T(8,128)(2,1)} %new_ref.3, bf16[80,32,2048]{2,1,0:T(8,128)(2,1)} %refs_2_.1), custom_call_target="tpu_custom_call" | custom-call | tf_op jit(solution)/shard_map/send_slots/pallas_call | solution.py:106
  3.0 2.2 %collective-permute-start = (bf16[2,64,2048]{2,1,0:T(8,128)(2,1)S(1)}, bf16[2,64,2048]{2,1,0:T(8,128)(2,1)S(1)}, u32[]{:S(2)}, u32[]{:S(2)}) collective-permute-start(bf16[2,64,2048]{2,1,0:T(8,128)(2,1)S(1)} %get-tuple-element.14), channel_id=1, source_target_pairs={{0,4},{1,5},{2,6},{3,7},{4,0},{5,1},{6,2},{7,3},{8,12},{9,13},{10,... | collective-permute-start | bytes 1572872 | tf_op jit(solution)/shard_map/ppermute | solution.py:303
  5.2 1.2 %collective-permute-start.2 = (bf16[2,64,2048]{2,1,0:T(8,128)(2,1)S(1)}, bf16[2,64,2048]{2,1,0:T(8,128)(2,1)S(1)}, u32[]{:S(2)}, u32[]{:S(2)}) collective-permute-start(bf16[2,64,2048]{2,1,0:T(8,128)(2,1)S(1)} %get-tuple-element.19), channel_id=1, source_target_pairs={{0,2},{1,3},{2,8},{3,1},{4,6},{5,7},{6,4},{7,13},{8,10},{9,11},{10... | collective-permute-start | bytes 1572872 | tf_op jit(solution)/shard_map/ppermute | solution.py:303
  6.4 1.2 %collective-permute-start.6 = (bf16[2,64,2048]{2,1,0:T(8,128)(2,1)S(1)}, bf16[2,64,2048]{2,1,0:T(8,128)(2,1)S(1)}, u32[]{:S(2)}, u32[]{:S(2)}) collective-permute-start(bf16[2,64,2048]{2,1,0:T(8,128)(2,1)S(1)} %get-tuple-element.22), channel_id=1, source_target_pairs={{0,8},{2,10},{4,12},{6,14},{8,16},{10,18},{12,20},{14,22},{16,24},... | collective-permute-start | bytes 1572872 | tf_op jit(solution)/shard_map/ppermute | solution.py:29
  7.7 0.0 copy-done.2
  7.7 5.7 %attention.2.refs_0_ = f32[16,2048]{1,0:T(8,128)S(1)} custom-call(s32[2,24]{1,0:T(2,128)S(1)} %copy-done.9, s32[2]{0:T(128)S(1)} %copy-done.10, s32[16]{0:T(128)S(1)} %copy-done.11, s32[2,16]{1,0:T(2,128)S(1)} %bitcast.5, s32[16]{0:T(128)S(1)} %copy-done.6, f32[4]{0:T(128)S(1)} %copy-done.12, bf16[16,1024]{1,0:T(8,128)(2,1)S(1)} %copy-done.2, ...), custom_call_target="tpu_custom_call" | custom-call | flops 201326592 | bytes 7340032 | tf_op jit(solution)/shard_map/attention/pallas_call | solution.py:223
  13.4 0.0 copy-start.1
  13.4 0.0 copy-start.5
  13.5 0.0 copy-start.7
  13.5 2.0 %send_slots.3 = bf16[2,64,2048]{2,1,0:T(8,128)(2,1)S(1)} custom-call(s32[2,16]{1,0:T(2,128)} %bitcast.4, s32[16]{0:T(128)} %cont_len.3, s32[2,6]{1,0:T(2,128)} %bitcast.9, bf16[16,2048]{1,0:T(8,128)(2,1)} %new_ref.3, bf16[80,32,2048]{2,1,0:T(8,128)(2,1)} %refs_2_.1), custom_call_target="tpu_custom_call" | custom-call | tf_op jit(solution)/shard_map/send_slots/pallas_call | solution.py:106
  15.4 0.0 copy-start.3
  15.5 0.0 copy-start.8
  15.5 1.4 %collective-permute-done.refs_0_ = bf16[2,64,2048]{2,1,0:T(8,128)(2,1)S(1)} collective-permute-done((bf16[2,64,2048]{2,1,0:T(8,128)(2,1)S(1)}, bf16[2,64,2048]{2,1,0:T(8,128)(2,1)S(1)}, u32[]{:S(2)}, u32[]{:S(2)}) %collective-permute-start) | collective-permute-done | bytes 524320 | tf_op jit(solution)/shard_map/ppermute | solution.py:303
  16.9 1.3 %collective-permute-start.5 = (bf16[2,64,2048]{2,1,0:T(8,128)(2,1)S(1)}, bf16[2,64,2048]{2,1,0:T(8,128)(2,1)S(1)}, u32[]{:S(2)}, u32[]{:S(2)}) collective-permute-start(bf16[2,64,2048]{2,1,0:T(8,128)(2,1)S(1)} %collective-permute-done.refs_0_), channel_id=1, source_target_pairs={{0,8},{1,9},{2,10},{3,11},{4,5},{5,4},{6,7},{7,6},{8,16},{9,17},{1... | collective-permute-start | bytes 1572872 | tf_op jit(solution)/shard_map/ppermute | solution.py:303
  18.1 2.3 %collective-permute-start.4 = (bf16[2,64,2048]{2,1,0:T(8,128)(2,1)S(1)}, bf16[2,64,2048]{2,1,0:T(8,128)(2,1)S(1)}, u32[]{:S(2)}, u32[]{:S(2)}) collective-permute-start(bf16[2,64,2048]{2,1,0:T(8,128)(2,1)S(1)} %send_slots.3), channel_id=1, source_target_pairs={{0,6},{1,7},{2,4},{3,5},{4,10},{5,11},{6,8},{7,9},{8,14},{9,15},{1... | collective-permute-start | bytes 1572872 | tf_op jit(solution)/shard_map/ppermute | solution.py:303
  20.5 0.0 collective-permute-done.2.refs_2_
  20.5 3.1 %collective-permute-start.3 = (bf16[2,64,2048]{2,1,0:T(8,128)(2,1)S(1)}, bf16[2,64,2048]{2,1,0:T(8,128)(2,1)S(1)}, u32[]{:S(2)}, u32[]{:S(2)}) collective-permute-start(bf16[2,64,2048]{2,1,0:T(8,128)(2,1)S(1)} %collective-permute-done.2.refs_2_), channel_id=1, source_target_pairs={{1,9},{4,12},{9,17},{12,20},{17,25},{20,28},{25,1},{28,4}} | collective-permute-start | bytes 1572872 | tf_op jit(solution)/shard_map/ppermute | solution.py:303
  23.7 5.7 %attention.3.refs_0_ = bf16[16,2048]{1,0:T(8,128)(2,1)S(1)} custom-call(s32[2,24]{1,0:T(2,128)S(1)} %copy-done.9, s32[2]{0:T(128)S(1)} %copy-done.10, s32[16]{0:T(128)S(1)} %copy-done.11, s32[2,16]{1,0:T(2,128)S(1)} %bitcast.6, s32[16]{0:T(128)S(1)} %copy-done.7, f32[4]{0:T(128)S(1)} %copy-done.12, bf16[16,1024]{1,0:T(8,128)(2,1)S(1)} %copy-done.2, ...), custom_call_target="tpu_custom_call" | custom-call | flops 201326592 | bytes 7340032 | tf_op jit(solution)/shard_map/attention/pallas_call | solution.py:223
  29.4 0.1 collective-permute-start.1
  29.5 1.2 %collective-permute-done.1.refs_1_ = bf16[16,2048]{1,0:T(8,128)(2,1)S(1)} collective-permute-done((bf16[16,2048]{1,0:T(8,128)(2,1)S(1)}, bf16[16,2048]{1,0:T(8,128)(2,1)S(1)}, u32[]{:S(2)}, u32[]{:S(2)}) %collective-permute-start.1) | collective-permute-done | bytes 65568 | tf_op jit(solution)/shard_map/ppermute | solution.py:29
  30.7 0.0 copy-done.8
  30.7 0.8 %finish.1 = (bf16[16,2048]{1,0:T(8,128)(2,1)}, bf16[16,2048]{1,0:T(8,128)(2,1)}) custom-call(bf16[16,2048]{1,0:T(8,128)(2,1)S(1)} %copy-done.3, f32[1,2048]{1,0:T(1,128)S(1)} %bitcast.7, bf16[16,2048]{1,0:T(8,128)(2,1)S(1)} %attention.3.refs_0_, bf16[16,2048]{1,0:T(8,128)(2,1)S(1)} %collective-permute-done.1.refs_1_), custom_call_target="tpu_custom_call" | custom-call | tf_op jit(solution)/shard_map/finish/pallas_call | solution.py:257
  31.5 0.0 collective-permute-done.6.refs_3_
  31.5 1.0 %collective-permute-done.5.refs_1_ = bf16[2,64,2048]{2,1,0:T(8,128)(2,1)S(1)} collective-permute-done((bf16[2,64,2048]{2,1,0:T(8,128)(2,1)S(1)}, bf16[2,64,2048]{2,1,0:T(8,128)(2,1)S(1)}, u32[]{:S(2)}, u32[]{:S(2)}) %collective-permute-start.5) | collective-permute-done | bytes 524320 | tf_op jit(solution)/shard_map/ppermute | solution.py:303
  32.5 1.0 %arrive.3.refs_1_ = bf16[8,64,2048]{2,1,0:T(8,128)(2,1)} custom-call(bf16[2,64,2048]{2,1,0:T(8,128)(2,1)S(1)} %collective-permute-done.refs_0_, bf16[2,64,2048]{2,1,0:T(8,128)(2,1)S(1)} %collective-permute-done.5.refs_1_, bf16[2,64,2048]{2,1,0:T(8,128)(2,1)S(1)} %collective-permute-done.2.refs_2_, bf16[2,64,2048]{2,1,0:T(8,128)(2,1)S(1)} %collective-permute-done.6.refs_3_), custom_call_target="tpu_custom_call" | custom-call | tf_op jit(solution)/shard_map/arrive/pallas_call | solution.py:282
  33.5 4.9 %collective-permute-done.4.refs_0_ = bf16[2,64,2048]{2,1,0:T(8,128)(2,1)S(1)} collective-permute-done((bf16[2,64,2048]{2,1,0:T(8,128)(2,1)S(1)}, bf16[2,64,2048]{2,1,0:T(8,128)(2,1)S(1)}, u32[]{:S(2)}, u32[]{:S(2)}) %collective-permute-start.4) | collective-permute-done | bytes 524320 | tf_op jit(solution)/shard_map/ppermute | solution.py:303
  38.4 0.9 %arrive.4.refs_1_ = bf16[8,64,2048]{2,1,0:T(8,128)(2,1)} custom-call(bf16[2,64,2048]{2,1,0:T(8,128)(2,1)S(1)} %collective-permute-done.4.refs_0_, bf16[8,64,2048]{2,1,0:T(8,128)(2,1)} %arrive.3.refs_1_), custom_call_target="tpu_custom_call", output_to_operand_aliasing={{}: (1, {})} | custom-call | tf_op jit(solution)/shard_map/arrive/pallas_call | solution.py:282
  39.3 0.0 collective-permute-done.3.refs_0_
  39.3 0.9 %arrive.5 = bf16[8,64,2048]{2,1,0:T(8,128)(2,1)} custom-call(bf16[2,64,2048]{2,1,0:T(8,128)(2,1)S(1)} %collective-permute-done.3.refs_0_, bf16[8,64,2048]{2,1,0:T(8,128)(2,1)} %arrive.4.refs_1_), custom_call_target="tpu_custom_call", output_to_operand_aliasing={{}: (1, {})} | custom-call | tf_op jit(solution)/shard_map/arrive/pallas_call | solution.py:282
  (16 shorter events, 0.0 us)
Async XLA Ops:
  0.6 7.0 %copy-start = (bf16[16,2048]{1,0:T(8,128)(2,1)S(1)}, bf16[16,2048]{1,0:T(8,128)(2,1)}, u32[]{:S(2)}) copy-start(bf16[16,2048]{1,0:T(8,128)(2,1)} %new_ref.3) | copy-start | bytes 196612
  0.6 7.0 %copy-start.2 = (bf16[16,1024]{1,0:T(8,128)(2,1)S(1)}, bf16[16,1024]{1,0:T(8,128)(2,1)}, u32[]{:S(2)}) copy-start(bf16[16,1024]{1,0:T(8,128)(2,1)} %query.3) | copy-start | bytes 98308
  0.7 7.0 %copy-start.4 = (s32[16,2]{0,1:T(2,128)S(1)}, s32[16,2]{0,1:T(2,128)}, u32[]{:S(2)}) copy-start(s32[16,2]{0,1:T(2,128)} %param.20) | copy-start | bytes 388
  0.7 7.0 %copy-start.6 = (s32[16]{0:T(128)S(1)}, s32[16]{0:T(128)}, u32[]{:S(2)}) copy-start(s32[16]{0:T(128)} %cont_len.3) | copy-start | bytes 196
  0.7 7.0 %copy-start.9 = (s32[2,24]{1,0:T(2,128)S(1)}, s32[2,24]{1,0:T(2,128)}, u32[]{:S(2)}) copy-start(s32[2,24]{1,0:T(2,128)} %prompt_table.3) | copy-start | bytes 580
  0.7 7.0 %copy-start.10 = (s32[2]{0:T(128)S(1)}, s32[2]{0:T(128)}, u32[]{:S(2)}) copy-start(s32[2]{0:T(128)} %prompt_len.3) | copy-start | bytes 28
  0.7 7.0 %copy-start.11 = (s32[16]{0:T(128)S(1)}, s32[16]{0:T(128)}, u32[]{:S(2)}) copy-start(s32[16]{0:T(128)} %req_group.3) | copy-start | bytes 196
  0.7 7.0 %copy-start.12 = (f32[4]{0:T(128)S(1)}, f32[4]{0:T(128)}, u32[]{:S(2)}) copy-start(f32[4]{0:T(128)} %lam.3) | copy-start | bytes 52
  3.0 13.8 %collective-permute-start = (bf16[2,64,2048]{2,1,0:T(8,128)(2,1)S(1)}, bf16[2,64,2048]{2,1,0:T(8,128)(2,1)S(1)}, u32[]{:S(2)}, u32[]{:S(2)}) collective-permute-start(bf16[2,64,2048]{2,1,0:T(8,128)(2,1)S(1)} %get-tuple-element.14), channel_id=1, source_target_pairs={{0,4},{1,5},{2,6},{3,7},{4,0},{5,1},{6,2},{7,3},{8,12},{9,13},{10,... | collective-permute-start | bytes 1572872 | tf_op jit(solution)/shard_map/ppermute | solution.py:303
  5.2 15.3 %collective-permute-start.2 = (bf16[2,64,2048]{2,1,0:T(8,128)(2,1)S(1)}, bf16[2,64,2048]{2,1,0:T(8,128)(2,1)S(1)}, u32[]{:S(2)}, u32[]{:S(2)}) collective-permute-start(bf16[2,64,2048]{2,1,0:T(8,128)(2,1)S(1)} %get-tuple-element.19), channel_id=1, source_target_pairs={{0,2},{1,3},{2,8},{3,1},{4,6},{5,7},{6,4},{7,13},{8,10},{9,11},{10... | collective-permute-start | bytes 1572872 | tf_op jit(solution)/shard_map/ppermute | solution.py:303
  6.4 25.0 %collective-permute-start.6 = (bf16[2,64,2048]{2,1,0:T(8,128)(2,1)S(1)}, bf16[2,64,2048]{2,1,0:T(8,128)(2,1)S(1)}, u32[]{:S(2)}, u32[]{:S(2)}) collective-permute-start(bf16[2,64,2048]{2,1,0:T(8,128)(2,1)S(1)} %get-tuple-element.22), channel_id=1, source_target_pairs={{0,8},{2,10},{4,12},{6,14},{8,16},{10,18},{12,20},{14,22},{16,24},... | collective-permute-start | bytes 1572872 | tf_op jit(solution)/shard_map/ppermute | solution.py:29
  13.4 10.2 %copy-start.1 = (bf16[16,2048]{1,0:T(8,128)(2,1)S(1)}, bf16[16,2048]{1,0:T(8,128)(2,1)}, u32[]{:S(2)}) copy-start(bf16[16,2048]{1,0:T(8,128)(2,1)} %new_ref.3) | copy-start | bytes 196612
  13.4 10.2 %copy-start.5 = (s32[16,2]{0,1:T(2,128)S(1)}, s32[16,2]{0,1:T(2,128)}, u32[]{:S(2)}) copy-start(s32[16,2]{0,1:T(2,128)} %param.20) | copy-start | bytes 388
  13.5 10.2 %copy-start.7 = (s32[16]{0:T(128)S(1)}, s32[16]{0:T(128)}, u32[]{:S(2)}) copy-start(s32[16]{0:T(128)} %cont_len.3) | copy-start | bytes 196
  15.4 15.3 %copy-start.3 = (bf16[16,2048]{1,0:T(8,128)(2,1)S(1)}, bf16[16,2048]{1,0:T(8,128)(2,1)}, u32[]{:S(2)}) copy-start(bf16[16,2048]{1,0:T(8,128)(2,1)} %hidden.1) | copy-start | bytes 196612
  15.5 15.2 %copy-start.8 = (f32[2048]{0:T(1024)S(1)}, f32[2048]{0:T(1024)}, u32[]{:S(2)}) copy-start(f32[2048]{0:T(1024)} %param.25) | copy-start | bytes 24580
  16.9 15.7 %collective-permute-start.5 = (bf16[2,64,2048]{2,1,0:T(8,128)(2,1)S(1)}, bf16[2,64,2048]{2,1,0:T(8,128)(2,1)S(1)}, u32[]{:S(2)}, u32[]{:S(2)}) collective-permute-start(bf16[2,64,2048]{2,1,0:T(8,128)(2,1)S(1)} %collective-permute-done.refs_0_), channel_id=1, source_target_pairs={{0,8},{1,9},{2,10},{3,11},{4,5},{5,4},{6,7},{7,6},{8,16},{9,17},{1... | collective-permute-start | bytes 1572872 | tf_op jit(solution)/shard_map/ppermute | solution.py:303
  18.1 20.3 %collective-permute-start.4 = (bf16[2,64,2048]{2,1,0:T(8,128)(2,1)S(1)}, bf16[2,64,2048]{2,1,0:T(8,128)(2,1)S(1)}, u32[]{:S(2)}, u32[]{:S(2)}) collective-permute-start(bf16[2,64,2048]{2,1,0:T(8,128)(2,1)S(1)} %send_slots.3), channel_id=1, source_target_pairs={{0,6},{1,7},{2,4},{3,5},{4,10},{5,11},{6,8},{7,9},{8,14},{9,15},{1... | collective-permute-start | bytes 1572872 | tf_op jit(solution)/shard_map/ppermute | solution.py:303
  20.5 18.8 %collective-permute-start.3 = (bf16[2,64,2048]{2,1,0:T(8,128)(2,1)S(1)}, bf16[2,64,2048]{2,1,0:T(8,128)(2,1)S(1)}, u32[]{:S(2)}, u32[]{:S(2)}) collective-permute-start(bf16[2,64,2048]{2,1,0:T(8,128)(2,1)S(1)} %collective-permute-done.2.refs_2_), channel_id=1, source_target_pairs={{1,9},{4,12},{9,17},{12,20},{17,25},{20,28},{25,1},{28,4}} | collective-permute-start | bytes 1572872 | tf_op jit(solution)/shard_map/ppermute | solution.py:303
  29.4 1.3 %collective-permute-start.1 = (bf16[16,2048]{1,0:T(8,128)(2,1)S(1)}, bf16[16,2048]{1,0:T(8,128)(2,1)S(1)}, u32[]{:S(2)}, u32[]{:S(2)}) collective-permute-start(bf16[16,2048]{1,0:T(8,128)(2,1)S(1)} %attention.3.refs_0_), channel_id=1, source_target_pairs={{0,1},{1,0},{2,3},{3,2},{4,5},{5,4},{6,7},{7,6},{8,9},{9,8},{10,11... | collective-permute-start | bytes 196616 | tf_op jit(solution)/shard_map/ppermute | solution.py:29
